TPU v7x, 256 devices: a whole 4x4x8 slice. The times are simulated.
256 devices in a mesh: gx: 16 (over y, z_lo), gy: 16 (over z_hi, x, core).
Axes of the slice: x: 4, y: 4, z: 8 (z_hi: 2, z_lo: 4; z = z_hi * 4 + z_lo), core: 2. Of those that a mesh axis runs over, the one named last changes fastest.
Arguments:
- latents: bfloat16 [16, 16, 512, 128], P('gx', 'gy'), may hold values from -6 to 6
- edge_latents: bfloat16 [16, 16, 4096, 128], P('gx', 'gy'), may hold values from -6 to 6
- senders: int32 [16, 16, 4096], P('gx', 'gy'), may hold values from 0 to 1663, as said below
- receivers: int32 [16, 16, 4096], P('gx', 'gy'), may hold values from 0 to 255
- ghost_rows: int32 [16, 16, 3, 3, 128], P('gx', 'gy'), may hold values from 0 to 511
- edge_count: int32 [16, 16], P('gx', 'gy'), may hold values from 1024 to 4096, as said below
- node_cotangent: bfloat16 [16, 16, 512, 128], P('gx', 'gy'), may hold values from -6 to 6
- edge_cotangent: bfloat16 [16, 16, 4096, 128], P('gx', 'gy'), may hold values from -6 to 6
- edge_first: bfloat16 [2, 384, 128], replicated, may hold values from -0.3125 to 0.3125
- edge_second: bfloat16 [2, 128, 128], replicated, may hold values from -0.5 to 0.5
- edge_scale: float32 [2, 128], replicated, may hold values from 0.5 to 1.5
- node_first: bfloat16 [2, 256, 128], replicated, may hold values from -0.375 to 0.375
- node_second: bfloat16 [2, 128, 128], replicated, may hold values from -0.5 to 0.5
- node_scale: float32 [2, 128], replicated, may hold values from 0.5 to 1.5
Outputs:
- nodes_out: bfloat16 [16, 16, 512, 128], P('gx', 'gy')
- edges_out: bfloat16 [16, 16, 4096, 128], P('gx', 'gy')
- latents_grad: float32 [16, 16, 512, 128], P('gx', 'gy')
- edge_latents_grad: float32 [16, 16, 4096, 128], P('gx', 'gy')
- edge_first_grad: float32 [2, 384, 128], replicated
- edge_second_grad: float32 [2, 128, 128], replicated
- edge_scale_grad: float32 [2, 128], replicated
- node_first_grad: float32 [2, 256, 128], replicated
- node_second_grad: float32 [2, 128, 128], replicated
- node_scale_grad: float32 [2, 128], replicated
Inputs may be any that keep to these rules, and one draw needn't show every extreme that they name: `senders`: rows 0 to 511 of the node table are the domain's particles; row 512 + k * 128 + j is ghost row j of slot k = 3 a + b, from the neighbour at offset (a - 1, b - 1); slot 4 is never named. `edge_count`: edge slots at positions below the count are live, later ones are padding.
All inputs are finite; a program needn't handle non-finite values.
Results may differ from a plain program's by a relative error of at most 0.02.
Values may be sent and summed in bfloat16 or wider, within the bound.
No kernel may reach another device: no remote copies, remote signals or barrier semaphores. Data moves between devices by JAX's collectives and lax.ppermute only.
A program may use at most 128 MiB of HBM per device.

v0:
```python
import functools

import jax
import jax.numpy as jnp
from jax import lax
from jax.experimental import pallas as pl
from jax.experimental.pallas import tpu as pltpu
from jax.sharding import PartitionSpec as P

L = 128
LAYERS = 2
TILE = 256
DEG = 8
G = 128
NODES = 512
EDGES = 4096
PART = TILE * DEG
BLOCK = 1024
BLOCKS = EDGES // BLOCK
PART_BLOCKS = PART // BLOCK
PACKED = 1024
OUTER = ((0, 0), (0, 1), (0, 2), (1, 0), (1, 2), (2, 0), (2, 1), (2, 2))

F32 = jnp.float32
BF16 = jnp.bfloat16
epsilon = 1e-05


def dot(a, b):
    return jnp.dot(a, b, preferred_element_type=F32)


def dot_nt(a, b):
    return lax.dot_general(a, b, (((1,), (1,)), ((), ())), preferred_element_type=F32)


def dot_tn(a, b):
    return lax.dot_general(a, b, (((0,), (0,)), ((), ())), preferred_element_type=F32)


def sigmoid(v):
    return 0.5 * jnp.tanh(0.5 * v) + 0.5


def column(row):
    parts = [
        jnp.transpose(jnp.broadcast_to(row[:, i : i + 128], (128, 128)))
        for i in range(0, row.shape[1], 128)
    ]
    return jnp.concatenate(parts, axis=0) if len(parts) > 1 else parts[0]


def hits(col, width):
    lane = lax.broadcasted_iota(jnp.int32, col.shape, 1)
    parts = [
        jnp.where(col == lane + 128 * t, 1.0, 0.0).astype(BF16) for t in range(width // 128)
    ]
    return jnp.concatenate(parts, axis=1)


def hits_t(row, height):
    sub = lax.broadcasted_iota(jnp.int32, (height, row.shape[1]), 0)
    return jnp.where(sub == row, 1.0, 0.0).astype(BF16)


def layer_norm(y):
    center = y - jnp.mean(y, axis=-1, keepdims=True)
    spread = jnp.mean(center * center, axis=-1, keepdims=True)
    rstd = lax.rsqrt(spread + epsilon)
    return center * rstd, rstd


def layer_norm_grad(dn, n, rstd):
    return rstd * (
        dn
        - jnp.mean(dn, axis=-1, keepdims=True)
        - n * jnp.mean(dn * n, axis=-1, keepdims=True)
    )


def silu_grad(z):
    s = sigmoid(z)
    return s * (1.0 + z * (1.0 - s))


def block_at(b):
    return pl.ds(pl.multiple_of(b * BLOCK, BLOCK), BLOCK)


def tile_at(b):
    return pl.ds(pl.multiple_of((b // PART_BLOCKS) * TILE, TILE), TILE)


def index_row(ref, b):
    return ref[:, block_at(b)]


def local_index(ids):
    return jnp.where(ids < TILE, ids, jnp.where(ids < NODES, ids - TILE, -1))


def ghost_index(ids):
    g = ids - NODES
    g = jnp.where(g >= 4 * G, g - G, g)
    return jnp.where(g >= NODES, g - NODES, g)


def ghost_upper(ids):
    return ids >= NODES + NODES + G


def live_of(b, count):
    slot = lax.broadcasted_iota(jnp.int32, (BLOCK, L), 0) + b * BLOCK
    return jnp.where(slot < count, 1.0, 0.0)


def pick(nodes_b, ghost_row_ref, slabs):
    rows = []
    for i, j in OUTER:
        col = column(ghost_row_ref[i, j : j + 1, :])
        rows.append(dot(hits(col, NODES), nodes_b).astype(BF16))
    put_slabs(rows, slabs)


def even_on(axis):
    return lax.rem(lax.axis_index(axis), 2) == 0


def put_slabs(rows, slabs):
    to_even, to_odd, same = slabs
    is_even = even_on("gx")
    for i in range(3):
        to_even[i] = jnp.where(is_even, rows[5 + i], rows[i])
        to_odd[i] = jnp.where(is_even, rows[i], rows[5 + i])
    same[0] = rows[3]
    same[1] = rows[4]


def from_both(is_even, even_ref, odd_ref, i):
    even, odd = even_ref[i], odd_ref[i]
    return jnp.where(is_even, odd, even), jnp.where(is_even, even, odd)


def arrived(refs):
    even_x, odd_x, even_y, odd_y = refs
    row = from_both(even_on("gx"), even_x, odd_x, 1)
    columns = [from_both(even_on("gy"), even_y, odd_y, i) for i in range(3)]
    return [
        columns[0][0], row[0], columns[0][1], columns[1][0], columns[1][1], columns[2][0], row[1],
        columns[2][1]
    ]


def local_pair(nodes_ref):
    return jnp.concatenate([nodes_ref[0:TILE, :], nodes_ref[TILE:NODES, :]], axis=1)


def ghost_pair(ghost_refs):
    rows = arrived(ghost_refs)
    lower = jnp.concatenate(rows[:4], axis=0)
    upper = jnp.concatenate(rows[4:], axis=0)
    return jnp.concatenate([lower, upper], axis=1)


def nodes_forward(nodes_b, inbound_b, u1, u2, gain):
    joined = jnp.concatenate([nodes_b, inbound_b], axis=1)
    z = dot(joined, u1)
    hidden = (z * sigmoid(z)).astype(BF16)
    n, rstd = layer_norm(dot(hidden, u2))
    nodes_next = (nodes_b.astype(F32) + n * gain).astype(BF16)
    return joined, z, hidden, n, rstd, nodes_next


def nodes_backward(grad, joined, z, hidden, n, rstd, u1, u2, gain, sums):
    sums[384:512, :] = dot_tn(hidden, (dy := layer_norm_grad(grad * gain, n, rstd).astype(BF16)))
    sums[513:514, :] = jnp.sum(grad * n, axis=0, keepdims=True)
    dz = (dot_nt(dy, u2).astype(BF16).astype(F32) * silu_grad(z)).astype(BF16)
    sums[128:384, :] = dot_tn(joined, dz)
    back = dot_nt(dz, u1).astype(BF16)
    return back[:, :L].astype(F32), back[:, L:]


def before_kernel(part, layer, nodes_ref, edges_ref, send_ref, recv_ref, w1_ref, sent_out,
                  received_out, z_out):
    pair = local_pair(nodes_ref)
    tile = nodes_ref[part * TILE : (part + 1) * TILE, :]
    w1 = w1_ref[layer]

    def step(i, carry):
        b = i + part * PART_BLOCKS
        ids = index_row(send_ref, b)
        both = dot(hits(column(local_index(ids)), TILE), pair)
        sent = jnp.where(column(ids) >= TILE, both[:, L:], both[:, :L]).astype(BF16)
        received = dot(hits(column(index_row(recv_ref, b)), TILE), tile).astype(BF16)
        sent_out[block_at(i), :] = sent
        received_out[block_at(i), :] = received
        joined = jnp.concatenate([sent, received, edges_ref[block_at(b), :]], axis=1)
        z_out[block_at(i), :] = dot(joined, w1)
        return carry

    lax.fori_loop(0, PART_BLOCKS, step, 0)


def edges_forward(b, local, count, table, edges_ref, send_ref, recv_ref, w1s, w2, gain, inbound,
                  edges_out, sent_out, z_out, n_out, rstd_out):
    sent_ref, z_ref, i = local
    ids = index_row(send_ref, b)
    both = dot(hits(column(ghost_index(ids)), NODES), table)
    sent = jnp.where(column(ids) >= 2 * NODES + G, both[:, L:], both[:, :L]).astype(BF16)
    z = z_ref[block_at(i), :] + dot(sent, w1s)
    hidden = (z * sigmoid(z)).astype(BF16)
    n, rstd = layer_norm(dot(hidden, w2))
    message = n * gain * live_of(b, count)
    at = block_at(b)
    edges_out[at, :] = (edges_ref[at, :].astype(F32) + message).astype(BF16)
    inbound[tile_at(b), :] += dot(hits_t(index_row(recv_ref, b), TILE), message.astype(BF16))
    sent_out[at, :] = sent_ref[block_at(i), :] + sent
    z_out[at, :] = z
    n_out[at, :] = n
    rstd_out[at, :] = jnp.broadcast_to(rstd, (BLOCK, L))


def all_edges_forward(count, locals_, ghost_refs, table, edges_ref, send_ref, recv_ref, w1s, w2,
                      gain, inbound, outs):
    table[...] = ghost_pair(ghost_refs)
    inbound[...] = jnp.zeros_like(inbound)
    for part in range(2):
        sent_ref, z_ref = locals_[2 * part : 2 * part + 2]

        def step(i, carry, part=part, sent_ref=sent_ref, z_ref=z_ref):
            edges_forward(
                i + part * PART_BLOCKS, (sent_ref, z_ref, i), count, table[...], edges_ref,
                send_ref, recv_ref, w1s, w2, gain, inbound, *outs
            )
            return carry

        lax.fori_loop(0, PART_BLOCKS, step, 0, unroll=True)


def edges_backward(b, count, grad_ref, dinbound, z_ref, n_ref, rstd_ref, send_ref, recv_ref, w1s,
                   w2, gain, dy_out, dz_out, dsent_out, gain_sum, dtable):
    at = block_at(b)
    n = n_ref[at, :]
    from_nodes = dot(hits(column(index_row(recv_ref, b)), TILE), dinbound[tile_at(b), :])
    dmessage = (grad_ref[at, :].astype(F32) + from_nodes) * live_of(b, count)
    gain_sum[0:1, :] += jnp.sum(dmessage * n, axis=0, keepdims=True)
    dy = layer_norm_grad(dmessage * gain, n, rstd_ref[at, :]).astype(BF16)
    dz = (dot_nt(dy, w2).astype(BF16).astype(F32) * silu_grad(z_ref[at, :])).astype(BF16)
    dsent = dot_nt(dz, w1s).astype(BF16)
    dy_out[at, :] = dy
    dz_out[at, :] = dz
    dsent_out[at, :] = dsent
    ids = index_row(send_ref, b)
    upper = column(ids) >= 2 * NODES + G
    dsent32 = dsent.astype(F32)
    pair = jnp.concatenate(
        [jnp.where(upper, 0.0, dsent32).astype(BF16), jnp.where(upper, dsent32, 0.0).astype(BF16)],
        axis=1,
    )
    dtable[...] += dot(hits_t(ghost_index(ids), NODES), pair)


def all_edges_backward(count, grad_ref, dinbound, residuals, send_ref, recv_ref, w1s, w2, gain,
                       outs, gain_sum, dtable, ghost_grad_out):
    gain_sum[...] = jnp.zeros_like(gain_sum)
    dtable[...] = jnp.zeros_like(dtable)

    def step(b, carry):
        edges_backward(
            b, count, grad_ref, dinbound, *residuals, send_ref, recv_ref, w1s, w2, gain, *outs,
            gain_sum, dtable
        )
        return carry

    lax.fori_loop(0, BLOCKS, step, 0, unroll=True)
    rows = []
    for s in range(8):
        at, half = pl.ds((s % 4) * G, G), pl.ds((s // 4) * L, L)
        rows.append(dtable[at, half].astype(BF16))
    put_slabs(rows, ghost_grad_out)


def add_weights(b, i, sent_ref, received_ref, edges_ref, z_ref, dy_ref, dz_ref, dw1, dw2):
    at = block_at(b)
    z = z_ref[at, :]
    dw2[...] += dot_tn((z * sigmoid(z)).astype(BF16), dy_ref[at, :])
    joined = jnp.concatenate(
        [sent_ref[at, :], received_ref[block_at(i), :], edges_ref[at, :]], axis=1
    )
    dw1[...] += dot_tn(joined, dz_ref[at, :])


def add_shares(b, dz_ref, dsent_ref, send_ref, recv_ref, w1re, edge_grad, dlocal, dtile):
    at = block_at(b)
    back = dot_nt(dz_ref[at, :], w1re).astype(BF16)
    dtile[...] += dot(hits_t(index_row(recv_ref, b), TILE), back[:, :L])
    ids = index_row(send_ref, b)
    upper = column(ids) >= TILE
    dsent32 = dsent_ref[at, :].astype(F32)
    pair = jnp.concatenate(
        [jnp.where(upper, 0.0, dsent32).astype(BF16), jnp.where(upper, dsent32, 0.0).astype(BF16)],
        axis=1,
    )
    dlocal[...] += dot(hits_t(local_index(ids), TILE), pair)
    return edge_grad + back[:, L:].astype(F32)


def pack(dw1, dw2, sums_ref, packed_out):
    gains = sums_ref[512:520, :]
    high = gains.astype(BF16).astype(F32)
    packed_out[0:384, :] = dw1[...].astype(BF16)
    packed_out[384:512, :] = dw2[...].astype(BF16)
    packed_out[512:896, :] = sums_ref[128:512, :].astype(BF16)
    packed_out[896:912, :] = jnp.concatenate([high, gains - high], axis=0).astype(BF16)
    packed_out[912:PACKED, :] = jnp.zeros((PACKED - 912, L), BF16)


def add_partial(partial_ref, dlocal, dtile0, dtile1, partial_out):
    partial_out[0:TILE, :] = partial_ref[0:TILE, :] + dtile0[...] + dlocal[:, :L]
    partial_out[TILE:, :] = partial_ref[TILE:, :] + dtile1[...] + dlocal[:, L:]


def after_kernel(part, layer, sent_ref, received_ref, edges_ref, z_ref, dy_ref, dz_ref, dsent_ref,
                 send_ref, recv_ref, w1_ref, edge_grad_ref, *rest):
    if part:
        dw1_in, dw2_in, dlocal_in, dtile_in, sums_ref, partial_ref = rest[:6]
        edge_grad_out, partial_out, packed_out, dw1, dw2, dlocal, dtile = rest[6:]
        dw1[...] = dw1_in[...]
        dw2[...] = dw2_in[...]
        dlocal[...] = dlocal_in[...]
    else:
        edge_grad_out, dw1, dw2, dlocal, dtile = rest
        dw1[...] = jnp.zeros_like(dw1)
        dw2[...] = jnp.zeros_like(dw2)
        dlocal[...] = jnp.zeros_like(dlocal)
    dtile[...] = jnp.zeros_like(dtile)
    w1re = w1_ref[layer, L:, :]

    def step(i, carry):
        b = i + part * PART_BLOCKS
        add_weights(b, i, sent_ref, received_ref, edges_ref, z_ref, dy_ref, dz_ref, dw1, dw2)
        grad = edge_grad_ref[block_at(b), :].astype(F32)
        grad = add_shares(b, dz_ref, dsent_ref, send_ref, recv_ref, w1re, grad, dlocal, dtile)
        edge_grad_out[block_at(i), :] = grad.astype(BF16)
        return carry

    lax.fori_loop(0, PART_BLOCKS, step, 0)
    if part:
        add_partial(partial_ref, dlocal, dtile_in, dtile, partial_out)
        pack(dw1, dw2, sums_ref, packed_out)


def weights_kernel(sent_ref, received0, received1, edges_ref, z_ref, dy_ref, dz_ref, sums_ref,
                   packed1_ref, packed_out, dw1, dw2):
    dw1[...] = jnp.zeros_like(dw1)
    dw2[...] = jnp.zeros_like(dw2)
    for part, received_ref in enumerate((received0, received1)):
        for i in range(PART_BLOCKS):
            add_weights(
                i + part * PART_BLOCKS, i, sent_ref, received_ref, edges_ref, z_ref, dy_ref, dz_ref,
                dw1, dw2
            )
    pack(dw1, dw2, sums_ref, packed_out)
    packed_out[PACKED:, :] = packed1_ref[...]


def shares_kernel(dz_ref, dsent_ref, send_ref, recv_ref, w1_ref, edge_grad0, edge_grad1,
                  partial_ref, edge_grad_out, partial_out, dlocal, dtile0, dtile1):
    dlocal[...] = jnp.zeros_like(dlocal)
    w1re = w1_ref[0, L:, :]
    for part, (edge_grad_ref, dtile) in enumerate(((edge_grad0, dtile0), (edge_grad1, dtile1))):
        dtile[...] = jnp.zeros_like(dtile)

        def step(i, carry, part=part, edge_grad_ref=edge_grad_ref, dtile=dtile):
            b = i + part * PART_BLOCKS
            edge_grad_out[block_at(b), :] = add_shares(
                b, dz_ref, dsent_ref, send_ref, recv_ref, w1re,
                edge_grad_ref[block_at(i), :].astype(F32), dlocal, dtile
            )
            return carry

        lax.fori_loop(0, PART_BLOCKS, step, 0)
    add_partial(partial_ref, dlocal, dtile0, dtile1, partial_out)


def pick_kernel(nodes_ref, ghost_row_ref, *slabs):
    pick(nodes_ref[...], ghost_row_ref, slabs)


def turn_kernel(even_x, odd_x, same, to_even, to_odd):
    rows = [from_both(even_on("gx"), even_x, odd_x, i) for i in (0, 2)]
    is_even = even_on("gy")
    left = (rows[0][0], same[0], rows[0][1])
    right = (rows[1][0], same[1], rows[1][1])
    for i in range(3):
        to_even[i] = jnp.where(is_even, right[i], left[i])
        to_odd[i] = jnp.where(is_even, left[i], right[i])


def first_kernel(
    count_ref, nodes_ref, edges_ref, send_ref, recv_ref, ghost_row_ref, w1_ref, w2_ref, g1_ref,
    u1_ref, u2_ref, g2_ref, sent0, z0, sent1, z1, *rest
):
    ghost_refs, rest = rest[:4], rest[4:]
    nodes_out, inbound_out, *slabs = rest[:5]
    outs, (table, inbound) = rest[5:10], rest[10:]
    all_edges_forward(
        count_ref[0, 0], (sent0, z0, sent1, z1), ghost_refs, table, edges_ref, send_ref, recv_ref,
        w1_ref[0, :L, :], w2_ref[0], g1_ref[0:1, :], inbound, outs
    )
    inbound_b = inbound[...].astype(BF16)
    inbound_out[...] = inbound_b
    nodes_next = nodes_forward(nodes_ref[...], inbound_b, u1_ref[0], u2_ref[0], g2_ref[0:1, :])[-1]
    nodes_out[...] = nodes_next
    pick(nodes_next, ghost_row_ref, slabs)


def start_nodes_backward(grad, nodes_b, inbound_b, layer, u1_ref, u2_ref, g2_ref, sums):
    u1, u2, gain = u1_ref[layer], u2_ref[layer], g2_ref[layer : layer + 1, :]
    sums[512:520, :] = jnp.zeros((8, L), F32)
    *saved, nodes_next = nodes_forward(nodes_b, inbound_b, u1, u2, gain)
    through, dinbound = nodes_backward(grad, *saved, u1, u2, gain, sums)
    return nodes_next, grad + through, dinbound


def middle_kernel(
    count_ref, nodes_ref, edges_ref, send_ref, recv_ref, w1_ref, w2_ref, g1_ref, u1_ref, u2_ref,
    g2_ref, node_grad_ref, edge_grad_ref, sent0, z0, sent1, z1, *rest
):
    ghost_refs, rest = rest[:4], rest[4:]
    nodes_out, edges_out, sent_out, z_out, dy_out, dz_out, dsent_out = rest[:7]
    partial_out, sums, *ghost_grad_out = rest[7:12]
    table, inbound, n_all, rstd_all, dinbound, dtable, gain_sum = rest[12:]
    count = count_ref[0, 0]
    w1s, w2, gain = w1_ref[1, :L, :], w2_ref[1], g1_ref[1:2, :]
    all_edges_forward(
        count, (sent0, z0, sent1, z1), ghost_refs, table, edges_ref, send_ref, recv_ref, w1s, w2,
        gain, inbound, (edges_out, sent_out, z_out, n_all, rstd_all)
    )
    nodes_out[...], partial_out[...], dinbound[...] = start_nodes_backward(
        node_grad_ref[...].astype(F32), nodes_ref[...], inbound[...].astype(BF16), 1, u1_ref,
        u2_ref, g2_ref, sums
    )
    all_edges_backward(
        count, edge_grad_ref, dinbound, (z_out, n_all, rstd_all), send_ref, recv_ref, w1s, w2, gain,
        (dy_out, dz_out, dsent_out), gain_sum, dtable, ghost_grad_out
    )
    sums[512:513, :] = gain_sum[0:1, :]


def last_kernel(
    count_ref, nodes_ref, inbound_ref, send_ref, recv_ref, ghost_row_ref, w1_ref, w2_ref, g1_ref,
    u1_ref, u2_ref, g2_ref, partial_ref, edge_grad0_ref, edge_grad1_ref, z_ref, n_ref, rstd_ref,
    *rest
):
    returned_refs, rest = rest[:4], rest[4:]
    dy_out, dz_out, dsent_out, partial_out, sums, *ghost_grad_out = rest[:8]
    dinbound, dtable, gain_sum, edge_grad = rest[8:]
    node_grad = add_returned(partial_ref[...], returned_refs, ghost_row_ref)
    _, partial_out[...], dinbound[...] = start_nodes_backward(
        node_grad.astype(BF16).astype(F32), nodes_ref[...], inbound_ref[...], 0, u1_ref, u2_ref,
        g2_ref, sums
    )
    edge_grad[0:PART, :] = edge_grad0_ref[...]
    edge_grad[PART:, :] = edge_grad1_ref[...]
    all_edges_backward(
        count_ref[0, 0], edge_grad, dinbound, (z_ref, n_ref, rstd_ref), send_ref, recv_ref,
        w1_ref[0, :L, :], w2_ref[0], g1_ref[0:1, :], (dy_out, dz_out, dsent_out), gain_sum, dtable,
        ghost_grad_out
    )
    sums[512:513, :] = gain_sum[0:1, :]


def add_returned(partial, returned_refs, ghost_row_ref):
    row = jnp.concatenate([ghost_row_ref[i, j : j + 1, :] for i, j in OUTER], axis=1)
    returned = jnp.concatenate(arrived(returned_refs), axis=0)
    return partial + dot(hits_t(row, NODES), returned)


def return_kernel(partial_ref, ghost_row_ref, *rest):
    rest[4][...] = add_returned(partial_ref[...], rest[:4], ghost_row_ref)


def call(kernel, name, outs, scratch, scalars, flops, *args):
    vmem = pl.BlockSpec(memory_space=pltpu.VMEM)
    smem = pl.BlockSpec(memory_space=pltpu.SMEM)
    return pl.pallas_call(
        kernel,
        name=name,
        out_shape=[jax.ShapeDtypeStruct(s, d) for s, d in outs],
        in_specs=[smem] * scalars + [vmem] * (len(args) - scalars),
        out_specs=[vmem] * len(outs),
        scratch_shapes=[pltpu.VMEM(s, d) for s, d in scratch],
        cost_estimate=pl.CostEstimate(flops=flops, bytes_accessed=1 << 20, transcendentals=0),
        compiler_params=pltpu.CompilerParams(vmem_limit_bytes=24 * 1024 * 1024),
    )(*args)


def swap(axis, to_even, to_odd):
    def pairs(first):
        ups = [(i, i + 1) for i in range(first, lax.axis_size(axis) - 1, 2)]
        return ups + [(j, i) for i, j in ups]

    odd = lax.ppermute(to_odd, axis, pairs(1))
    return lax.ppermute(to_even, axis, pairs(0)), odd


def turn(even_x, odd_x, same):
    outs = [(even_x.shape, BF16)] * 2
    return call(turn_kernel, "turn", outs, [], 0, 10**6, even_x, odd_x, same)


def exchange(slabs, beside):
    to_even, to_odd, same = slabs
    even_x, odd_x = swap("gx", to_even, to_odd)
    first = beside(0, None)
    to_even, to_odd = turn(even_x, odd_x, same)
    even_y, odd_y = swap("gy", to_even, to_odd)
    second = beside(1, (first, to_even))
    return (even_x, odd_x, even_y, odd_y), first, second


def sum_over_domains(packed, slabs, late):
    axes = ("gx", "gy")
    plane, line = planes_and_lines(lax.axis_size("gx"), lax.axis_size("gy"))
    hold = lax.optimization_barrier

    def trade(parts, groups):
        return lax.all_to_all(parts, axes, 0, 0, tiled=True, axis_index_groups=groups)

    def copies(parts, groups):
        shape = (len(groups[0]),) + parts.shape[1:]
        return call(spread_kernel, "spread", [(shape, BF16)], [], 0, 10**6, parts)[0]

    to_even, to_odd, same = slabs
    packed, to_even, to_odd = hold((packed.reshape(len(plane[0]), -1, L), to_even, to_odd))
    parts = trade(packed, plane)
    parts, even_x, odd_x = hold((parts, *swap("gx", to_even, to_odd)))
    parts, same = hold((copies(parts, line), same))
    parts = trade(parts, line)
    parts, even_y, odd_y = hold((parts, *swap("gy", *turn(even_x, odd_x, same))))
    parts, late = hold((copies(parts, plane), late))
    total = trade(parts, plane).reshape(LAYERS, PACKED, L)
    return total, (even_x, odd_x, even_y, odd_y), late


def planes_and_lines(rows, columns):
    planes, lines = {}, {}
    for i in range(rows * columns):
        gx, gy = divmod(i, columns)
        y, z_low = divmod(gx, 4)
        z_high, rest = divmod(gy, 8)
        planes.setdefault((z_high, z_low), []).append(i)
        lines.setdefault((y, rest), []).append(i)
    return list(planes.values()), list(lines.values())


def spread_kernel(parts_ref, copies_out):
    total = parts_ref[0].astype(F32)
    for k in range(1, parts_ref.shape[0]):
        total = total + parts_ref[k].astype(F32)
    for k in range(copies_out.shape[0]):
        copies_out[k] = total.astype(BF16)


def unpack_kernel(total_ref, dw1, dw2, dg1, du1, du2, dg2):
    for i in range(LAYERS):
        dw1[i] = total_ref[i, 0:384, :].astype(F32)
        dw2[i] = total_ref[i, 384:512, :].astype(F32)
        du1[i] = total_ref[i, 512:768, :].astype(F32)
        du2[i] = total_ref[i, 768:896, :].astype(F32)
        gains = total_ref[i, 896:912, :].astype(F32)
        dg1[i : i + 1, :] = gains[0:1, :] + gains[8:9, :]
        dg2[i : i + 1, :] = gains[1:2, :] + gains[9:10, :]


def on_device(
    latents,
    edge_latents,
    senders,
    receivers,
    ghost_rows,
    edge_count,
    node_cotangent,
    edge_cotangent,
    edge_first,
    edge_second,
    edge_scale,
    node_first,
    node_second,
    node_scale,
):
    nodes0 = latents[0, 0]
    edges0 = edge_latents[0, 0]
    ids = senders[0]
    targets = receivers[0]
    grow = ghost_rows[0, 0]
    weights = (edge_first, edge_second, edge_scale, node_first, node_second, node_scale)

    node_b = ((NODES, L), BF16)
    node_f = ((NODES, L), F32)
    edge_b = ((EDGES, L), BF16)
    edge_f = ((EDGES, L), F32)
    part_b = ((PART, L), BF16)
    part_f = ((PART, L), F32)
    slabs_b = [((n, G, L), BF16) for n in (3, 3, 2)]
    packed_b = ((PACKED, L), BF16)
    sums_f = ((520, L), F32)
    pair_b = ((NODES, 2 * L), BF16)
    pair_f = ((NODES, 2 * L), F32)
    gain_f = ((8, L), F32)
    dw1_f = ((3 * L, L), F32)
    dw2_f = ((L, L), F32)
    dlocal_f = ((TILE, 2 * L), F32)
    dtile_f = ((TILE, L), F32)

    def before(layer, nodes, edges):
        def part_of(part, wait):
            node_arg = nodes
            if wait is not None:
                node_arg, _ = lax.optimization_barrier((nodes, wait))
            return call(
                functools.partial(before_kernel, part, layer), f"before{layer}{part}",
                [part_b, part_b, part_f], [], 0, 2 * 10**9, node_arg, edges, ids, targets,
                edge_first
            )

        return part_of

    def after(layer, sent, received, edges, z, dy, dz, dsent, edge_grads, sums, partial):
        def part_of(part, wait):
            dy_arg, extra = dy, ()
            if part:
                dy_arg, _ = lax.optimization_barrier((dy, wait[1]))
                extra = (*wait[0][1:], sums, partial)
            outs = [part_b]
            outs += [node_f, packed_b] if part else [dw1_f, dw2_f, dlocal_f, dtile_f]
            return call(
                functools.partial(after_kernel, part, layer), f"after{layer}{part}", outs,
                [dw1_f, dw2_f, dlocal_f, dtile_f] if part else [], 0, 2 * 10**9, sent,
                received[part], edges, z, dy_arg, dz, dsent, ids, targets, edge_first, edge_grads,
                *extra
            )

        return part_of

    picked = call(pick_kernel, "pick", slabs_b, [], 0, 10**8, nodes0, grow)
    ghosts, a0, a1 = exchange(picked, before(0, nodes0, edges0))
    nodes1, inbound, *picked, edges1, sent_0, z_0, n_0, rstd_0 = call(
        first_kernel, "first", [node_b, node_b, *slabs_b, edge_b, edge_b, edge_f, edge_f, edge_f],
        [pair_b, node_f], 1, 4 * 10**9, edge_count, nodes0, edges0, ids, targets, grow, *weights,
        a0[0], a0[2], a1[0], a1[2], *ghosts
    )
    received_0 = (a0[1], a1[1])
    ghosts, a0, a1 = exchange(picked, before(1, nodes1, edges1))
    received_1 = (a0[1], a1[1])
    nodes2, edges2, sent_1, z_1, dy, dz, dsent, partial, sums, *ghost_grad = call(
        middle_kernel, "middle",
        [node_b, edge_b, edge_b, edge_f, edge_b, edge_b, edge_b, node_f, sums_f, *slabs_b],
        [pair_b, node_f, edge_f, edge_f, node_b, pair_f, gain_f], 1, 8 * 10**9, edge_count, nodes1,
        edges1, ids, targets, *weights, node_cotangent[0, 0], edge_cotangent[0, 0], a0[0], a0[2],
        a1[0], a1[2], *ghosts
    )
    returned, c0, c1 = exchange(
        ghost_grad,
        after(1, sent_1, received_1, edges1, z_1, dy, dz, dsent, edge_cotangent[0, 0], sums, partial),
    )
    edge_grad0, (edge_grad1, partial, packed1) = c0[0], c1
    dy, dz, dsent, partial, sums, *ghost_grad = call(
        last_kernel, "last", [edge_b, edge_b, edge_b, node_f, sums_f, *slabs_b],
        [node_b, pair_f, gain_f, edge_b], 1, 4 * 10**9, edge_count, nodes0, inbound, ids, targets,
        grow, *weights, partial, edge_grad0, edge_grad1, z_0, n_0, rstd_0, *returned
    )
    (packed,) = call(
        weights_kernel, "weights", [((LAYERS * PACKED, L), BF16)], [dw1_f, dw2_f], 0, 2 * 10**9,
        sent_0, *received_0, edges0, z_0, dy, dz, sums, packed1
    )
    total, returned, dsent = sum_over_domains(packed, ghost_grad, dsent)
    edge_grad, partial = call(
        shares_kernel, "shares", [edge_f, node_f], [dlocal_f, dtile_f, dtile_f], 0, 2 * 10**9, dz,
        dsent, ids, targets, edge_first, edge_grad0, edge_grad1, partial
    )
    (node_grad,) = call(
        return_kernel, "returned", [node_f], [], 0, 10**8, partial, grow, *returned
    )
    grads = call(
        unpack_kernel, "unpack", [((LAYERS,) + w.shape[1:], F32) for w in weights], [], 0, 10**6,
        total
    )
    return (
        nodes2[None, None],
        edges2[None, None],
        node_grad[None, None],
        edge_grad[None, None],
        *grads,
    )


def solution(mesh):
    domain = P("gx", "gy", None, None)
    placed = (
        domain,
        domain,
        P("gx", "gy", None),
        P("gx", "gy", None),
        P("gx", "gy", None, None, None),
        P("gx", "gy"),
        domain,
        domain,
        P(),
        P(),
        P(),
        P(),
        P(),
        P(),
    )
    return jax.shard_map(
        on_device,
        mesh=mesh,
        in_specs=placed,
        out_specs=(domain, domain, domain, domain, P(), P(), P(), P(), P(), P()),
        check_vma=False,
    )
```

profile of v0, /device:TPU:1, one launch (start us, length us, event | category | flops | bytes accessed | tf_op | source)
XLA Modules:
  0.0 152.0 jit_solution(6142450993714693227)
XLA Ops:
  0.6 0.7 copy.26
  1.3 0.9 copy-done.10
  2.2 0.5 pick.1
  2.7 2.6 %collective-permute-start = (bf16[3,128,128]{2,1,0:T(8,128)(2,1)S(1)}, bf16[3,128,128]{2,1,0:T(8,128)(2,1)S(1)}, u32[]{:S(2)}, u32[]{:S(2)}) collective-permute-start(bf16[3,128,128]{2,1,0:T(8,128)(2,1)S(1)} %get-tuple-element.98), channel_id=1, source_target_pairs={{0,16},{32,48},{64,80},{96,112},{128,144},{160,176},{192,208},{224... | collective-permute-start | bytes 294920 | tf_op jit(solution)/shard_map/ppermute | solution.py:505
  5.3 0.7 collective-permute-start.1
  6.6 0.0 copy-start.1
  6.6 1.2 copy-done.1
  7.8 0.9 copy-done.3
  8.8 0.7 copy-done.5
  9.5 0.7 copy-done.7
  10.2 1.4 before00.1
  11.6 0.1 turn.4
  11.7 4.0 %collective-permute-start.3 = (bf16[3,128,128]{2,1,0:T(8,128)(2,1)S(1)}, bf16[3,128,128]{2,1,0:T(8,128)(2,1)S(1)}, u32[]{:S(2)}, u32[]{:S(2)}) collective-permute-start(bf16[3,128,128]{2,1,0:T(8,128)(2,1)S(1)} %get-tuple-element.105), channel_id=1, source_target_pairs={{1,2},{3,4},{5,6},{7,8},{9,10},{11,12},{13,14},{2,1},{4,3},{6,5},{... | collective-permute-start | bytes 294920 | tf_op jit(solution)/shard_map/ppermute | solution.py:504
  15.7 0.1 collective-permute-start.2
  15.8 0.0 copy-start.12
  15.8 0.0 copy-start.15
  15.8 0.0 copy-start.16
  15.8 1.4 before01.1
  17.3 0.7 collective-permute-done.3.rest_3_
  18.0 6.0 %first.1 = (bf16[512,128]{1,0:T(8,128)(2,1)S(1)}, bf16[512,128]{1,0:T(8,128)(2,1)S(1)}, bf16[3,128,128]{2,1,0:T(8,128)(2,1)S(1)}, bf16[3,128,128]{2,1,0:T(8,128)...) custom-call(s32[1,1]{1,0:T(1,128)S(6)} %copy.27.count_ref, ...), custom_call_target="tpu_custom_call" | custom-call | flops 4000000000 | bytes 1048576 | tf_op jit(solution)/shard_map/first/pallas_call | solution.py:487
  24.0 4.9 %collective-permute-start.4 = (bf16[3,128,128]{2,1,0:T(8,128)(2,1)S(1)}, bf16[3,128,128]{2,1,0:T(8,128)(2,1)S(1)}, u32[]{:S(2)}, u32[]{:S(2)}) collective-permute-start(bf16[3,128,128]{2,1,0:T(8,128)(2,1)S(1)} %get-tuple-element.111), channel_id=1, source_target_pairs={{0,16},{32,48},{64,80},{96,112},{128,144},{160,176},{192,208},{224... | collective-permute-start | bytes 294920 | tf_op jit(solution)/shard_map/ppermute | solution.py:505
  28.9 0.7 collective-permute-start.5
  29.6 1.4 before10.1
  31.0 1.3 collective-permute-done.4.even_x.rest_0_
  32.3 0.1 turn.5
  32.3 3.7 %collective-permute-start.7 = (bf16[3,128,128]{2,1,0:T(8,128)(2,1)S(1)}, bf16[3,128,128]{2,1,0:T(8,128)(2,1)S(1)}, u32[]{:S(2)}, u32[]{:S(2)}) collective-permute-start(bf16[3,128,128]{2,1,0:T(8,128)(2,1)S(1)} %get-tuple-element.118), channel_id=1, source_target_pairs={{1,2},{3,4},{5,6},{7,8},{9,10},{11,12},{13,14},{2,1},{4,3},{6,5},{... | collective-permute-start | bytes 294920 | tf_op jit(solution)/shard_map/ppermute | solution.py:504
  36.0 0.3 collective-permute-start.6
  36.3 0.0 copy-start
  36.3 1.4 before11.1
  37.7 0.5 collective-permute-done.7.rest_3_
  38.3 0.0 copy-start.4
  38.3 9.9 %middle.1 = (bf16[512,128]{1,0:T(8,128)(2,1)}, bf16[4096,128]{1,0:T(8,128)(2,1)}, bf16[4096,128]{1,0:T(8,128)(2,1)S(1)}, f32[4096,128]{1,0:T(8,128)S(1)}, bf16[4...) custom-call(s32[1,1]{1,0:T(1,128)S(6)} %copy.27.count_ref, ...), custom_call_target="tpu_custom_call" | custom-call | flops 8000000000 | bytes 1048576 | tf_op jit(solution)/shard_map/middle/pallas_call | solution.py:487
  48.2 3.5 %collective-permute-start.8 = (bf16[3,128,128]{2,1,0:T(8,128)(2,1)S(1)}, bf16[3,128,128]{2,1,0:T(8,128)(2,1)S(1)}, u32[]{:S(2)}, u32[]{:S(2)}) collective-permute-start(bf16[3,128,128]{2,1,0:T(8,128)(2,1)S(1)} %get-tuple-element.126), channel_id=1, source_target_pairs={{0,16},{32,48},{64,80},{96,112},{128,144},{160,176},{192,208},{224... | collective-permute-start | bytes 294920 | tf_op jit(solution)/shard_map/ppermute | solution.py:505
  51.6 0.7 collective-permute-start.9
  52.3 2.1 %after10.1 = (bf16[2048,128]{1,0:T(8,128)(2,1)S(1)}, f32[384,128]{1,0:T(8,128)S(1)}, f32[128,128]{1,0:T(8,128)S(1)}, f32[256,256]{1,0:T(8,128)S(1)}, f32[256,128]{1,0:T(8,128)S(1)}) custom-call(bf16[4096,128]{1,0:T(8,128)(2,1)S(1)} %get-tuple-element.122.sent_ref, bf16[2048,128]{1,0:T(8,128)(2,1)S(1)} %get-tuple-element.110.received_ref, ...), custom_call_target="tpu_custom_call" | custom-call | flops 2000000000 | bytes 1048576 | tf_op jit(solution)/shard_map/after10/pallas_call | solution.py:487
  54.3 0.5 collective-permute-done.8.even_x.rest_0_
  54.8 0.1 turn.6
  54.9 0.8 collective-permute-start.10
  55.7 3.1 %collective-permute-start.11 = (bf16[3,128,128]{2,1,0:T(8,128)(2,1)S(1)}, bf16[3,128,128]{2,1,0:T(8,128)(2,1)S(1)}, u32[]{:S(2)}, u32[]{:S(2)}) collective-permute-start(bf16[3,128,128]{2,1,0:T(8,128)(2,1)S(1)} %get-tuple-element.145), channel_id=1, source_target_pairs={{1,2},{3,4},{5,6},{7,8},{9,10},{11,12},{13,14},{2,1},{4,3},{6,5},{... | collective-permute-start | bytes 294920 | tf_op jit(solution)/shard_map/ppermute | solution.py:504
  58.9 2.1 %after11.1 = (bf16[2048,128]{1,0:T(8,128)(2,1)S(1)}, f32[512,128]{1,0:T(8,128)S(1)}, bf16[1024,128]{1,0:T(8,128)(2,1)S(1)}) custom-call(bf16[4096,128]{1,0:T(8,128)(2,1)S(1)} %get-tuple-element.122.sent_ref, bf16[2048,128]{1,0:T(8,128)(2,1)S(1)} %get-tuple-element.123.received_ref, bf16[4096,128]{1,0:T(8,128)(2,1)S(1)} %get-tuple-element.107.edges_ref, ...), custom_call_target="tpu_custom_call" | custom-call | flops 2000000000 | bytes 1048576 | tf_op jit(solution)/shard_map/after11/pallas_call | solution.py:487
  61.0 0.7 collective-permute-done.11.rest_3_
  61.7 5.5 %last.1 = (bf16[4096,128]{1,0:T(8,128)(2,1)S(1)}, bf16[4096,128]{1,0:T(8,128)(2,1)S(1)}, bf16[4096,128]{1,0:T(8,128)(2,1)S(1)}, f32[512,128]{1,0:T(8,128)S(1)}, ...) custom-call(s32[1,1]{1,0:T(1,128)S(6)} %copy.27.count_ref, ...), custom_call_target="tpu_custom_call" | custom-call | flops 4000000000 | bytes 1048576 | tf_op jit(solution)/shard_map/last/pallas_call | solution.py:487
  67.2 0.0 copy-start.17
  67.2 1.0 copy-done.17
  68.2 2.2 %weights.1 = bf16[2048,128]{1,0:T(8,128)(2,1)} custom-call(bf16[4096,128]{1,0:T(8,128)(2,1)S(1)} %get-tuple-element.147.sent_ref, bf16[2048,128]{1,0:T(8,128)(2,1)S(1)} %get-tuple-element.97.received0, bf16[2048,128]{1,0:T(8,128)(2,1)S(1)} %get-tuple-element.148.received1, bf16[4096,128]{1,0:T(8,128)(2,1)S(1)} %bitcast.22, ...), custom_call_target="tpu_custom_call" | custom-call | flops 2000000000 | bytes 1048576 | tf_op jit(solution)/shard_map/weights/pallas_call | solution.py:487
  70.3 31.3 %all-to-all-start = ((bf16[32,64,128]{2,1,0:T(8,128)(2,1)}), bf16[32,64,128]{2,1,0:T(8,128)(2,1)S(1)}, u32[]{:S(2)}, u32[]{:S(2)}) async-start(bf16[32,64,128]{2,1,0:T(8,128)(2,1)} %bitcast.8), calls=%async_computation | async-start | bytes 1048576 | tf_op jit(solution)/shard_map/all_to_all | solution.py:529
  101.7 0.5 collective-permute-start.12
  102.1 0.7 collective-permute-start.13
  102.8 3.1 %collective-permute-done.12.even_x.rest_0_ = bf16[3,128,128]{2,1,0:T(8,128)(2,1)S(1)} collective-permute-done((bf16[3,128,128]{2,1,0:T(8,128)(2,1)S(1)}, bf16[3,128,128]{2,1,0:T(8,128)(2,1)S(1)}, u32[]{:S(2)}, u32[]{:S(2)}) %collective-permute-start.12) | collective-permute-done | bytes 98336 | tf_op jit(solution)/shard_map/ppermute | solution.py:505
  105.9 7.8 %all-to-all-done.parts_ref = bf16[32,64,128]{2,1,0:T(8,128)(2,1)S(1)} async-done(((bf16[32,64,128]{2,1,0:T(8,128)(2,1)}), bf16[32,64,128]{2,1,0:T(8,128)(2,1)S(1)}, u32[]{:S(2)}, u32[]{:S(2)}) %all-to-all-start) | async-done | bytes 524320 | tf_op jit(solution)/shard_map/all_to_all | solution.py:529
  113.7 0.7 spread.2
  114.5 6.0 %all-to-all-start.1 = ((bf16[8,64,128]{2,1,0:T(8,128)(2,1)}), bf16[8,64,128]{2,1,0:T(8,128)(2,1)S(1)}, u32[]{:S(2)}, u32[]{:S(2)}) async-start(bf16[8,64,128]{2,1,0:T(8,128)(2,1)} %spread.2), calls=%async_computation.1 | async-start | bytes 262144 | tf_op jit(solution)/shard_map/all_to_all | solution.py:529
  120.5 0.1 turn.7
  120.5 0.7 collective-permute-start.14
  121.2 2.5 %collective-permute-start.15 = (bf16[3,128,128]{2,1,0:T(8,128)(2,1)S(1)}, bf16[3,128,128]{2,1,0:T(8,128)(2,1)S(1)}, u32[]{:S(2)}, u32[]{:S(2)}) collective-permute-start(bf16[3,128,128]{2,1,0:T(8,128)(2,1)S(1)} %get-tuple-element.164), channel_id=1, source_target_pairs={{1,2},{3,4},{5,6},{7,8},{9,10},{11,12},{13,14},{2,1},{4,3},{6,5},{... | collective-permute-start | bytes 294920 | tf_op jit(solution)/shard_map/ppermute | solution.py:504
  123.8 3.7 %collective-permute-done.15.rest_3_ = bf16[3,128,128]{2,1,0:T(8,128)(2,1)S(1)} collective-permute-done((bf16[3,128,128]{2,1,0:T(8,128)(2,1)S(1)}, bf16[3,128,128]{2,1,0:T(8,128)(2,1)S(1)}, u32[]{:S(2)}, u32[]{:S(2)}) %collective-permute-start.15) | collective-permute-done | bytes 98336 | tf_op jit(solution)/shard_map/ppermute | solution.py:504
  127.5 0.9 spread.3
  128.3 11.2 %all-to-all-start.2 = ((bf16[32,64,128]{2,1,0:T(8,128)(2,1)}), bf16[32,64,128]{2,1,0:T(8,128)(2,1)S(1)}, u32[]{:S(2)}, u32[]{:S(2)}) async-start(bf16[32,64,128]{2,1,0:T(8,128)(2,1)} %spread.3), calls=%async_computation.2 | async-start | bytes 1048576 | tf_op jit(solution)/shard_map/all_to_all | solution.py:529
  139.6 0.0 copy-start.18
  139.6 1.2 copy-done.18
  140.8 4.5 %shares.1 = (f32[4096,128]{1,0:T(8,128)}, f32[512,128]{1,0:T(8,128)S(1)}) custom-call(bf16[4096,128]{1,0:T(8,128)(2,1)S(1)} %get-tuple-element.146.dz_ref, bf16[4096,128]{1,0:T(8,128)(2,1)S(1)} %copy-done.18, s32[1,4096]{1,0:T(1,128)S(1)} %bitcast.32, s32[1,4096]{1,0:T(1,128)S(1)} %bitcast.42, bf16[2,384,128]{2,1,0:T(8,128)(2,1)S(1)} %copy-done.4, ...), custom_call_target="tpu_custom_call" | custom-call | flops 2000000000 | bytes 1048576 | tf_op jit(solution)/shard_map/shares/pallas_call | solution.py:487
  145.2 1.2 returned.1
  146.4 4.7 %all-to-all-done.2 = bf16[32,64,128]{2,1,0:T(8,128)(2,1)S(1)} async-done(((bf16[32,64,128]{2,1,0:T(8,128)(2,1)}), bf16[32,64,128]{2,1,0:T(8,128)(2,1)S(1)}, u32[]{:S(2)}, u32[]{:S(2)}) %all-to-all-start.2) | async-done | bytes 524320 | tf_op jit(solution)/shard_map/all_to_all | solution.py:529
  151.1 0.9 unpack.1
  (37 shorter events, 0.1 us)
Async XLA Ops:
  1.3 0.9 copy-start.10
  2.7 8.9 %collective-permute-start = (bf16[3,128,128]{2,1,0:T(8,128)(2,1)S(1)}, bf16[3,128,128]{2,1,0:T(8,128)(2,1)S(1)}, u32[]{:S(2)}, u32[]{:S(2)}) collective-permute-start(bf16[3,128,128]{2,1,0:T(8,128)(2,1)S(1)} %get-tuple-element.98), channel_id=1, source_target_pairs={{0,16},{32,48},{64,80},{96,112},{128,144},{160,176},{192,208},{224... | collective-permute-start | bytes 294920 | tf_op jit(solution)/shard_map/ppermute | solution.py:505
  5.3 6.3 %collective-permute-start.1 = (bf16[3,128,128]{2,1,0:T(8,128)(2,1)S(1)}, bf16[3,128,128]{2,1,0:T(8,128)(2,1)S(1)}, u32[]{:S(2)}, u32[]{:S(2)}) collective-permute-start(bf16[3,128,128]{2,1,0:T(8,128)(2,1)S(1)} %get-tuple-element.99), channel_id=1, source_target_pairs={{16,32},{48,64},{80,96},{112,128},{144,160},{176,192},{208,224},{3... | collective-permute-start | bytes 294920 | tf_op jit(solution)/shard_map/ppermute | solution.py:504
  6.6 1.2 copy-start.1
  7.8 0.9 copy-start.3
  8.8 0.7 copy-start.5
  9.5 0.7 copy-start.7
  10.2 5.6 %copy-start.2 = (bf16[1,1,4096,128]{3,2,1,0:T(8,128)(2,1)S(1)}, bf16[1,1,4096,128]{3,2,1,0:T(8,128)(2,1)}, u32[]{:S(2)}) copy-start(bf16[1,1,4096,128]{3,2,1,0:T(8,128)(2,1)} %param.15) | copy-start | bytes 3145732
  11.7 6.2 %collective-permute-start.3 = (bf16[3,128,128]{2,1,0:T(8,128)(2,1)S(1)}, bf16[3,128,128]{2,1,0:T(8,128)(2,1)S(1)}, u32[]{:S(2)}, u32[]{:S(2)}) collective-permute-start(bf16[3,128,128]{2,1,0:T(8,128)(2,1)S(1)} %get-tuple-element.105), channel_id=1, source_target_pairs={{1,2},{3,4},{5,6},{7,8},{9,10},{11,12},{13,14},{2,1},{4,3},{6,5},{... | collective-permute-start | bytes 294920 | tf_op jit(solution)/shard_map/ppermute | solution.py:504
  15.7 2.3 %collective-permute-start.2 = (bf16[3,128,128]{2,1,0:T(8,128)(2,1)S(1)}, bf16[3,128,128]{2,1,0:T(8,128)(2,1)S(1)}, u32[]{:S(2)}, u32[]{:S(2)}) collective-permute-start(bf16[3,128,128]{2,1,0:T(8,128)(2,1)S(1)} %get-tuple-element.101), channel_id=1, source_target_pairs={{0,1},{2,3},{4,5},{6,7},{8,9},{10,11},{12,13},{14,15},{1,0},{3,2},... | collective-permute-start | bytes 294920 | tf_op jit(solution)/shard_map/ppermute | solution.py:505
  15.8 2.2 %copy-start.12 = (bf16[2,256,128]{2,1,0:T(8,128)(2,1)S(1)}, bf16[2,256,128]{2,1,0:T(8,128)(2,1)}, u32[]{:S(2)}) copy-start(bf16[2,256,128]{2,1,0:T(8,128)(2,1)} %u1_ref.5) | copy-start | bytes 393220
  15.8 2.2 %copy-start.13 = (bf16[2,128,128]{2,1,0:T(8,128)(2,1)S(1)}, bf16[2,128,128]{2,1,0:T(8,128)(2,1)}, u32[]{:S(2)}) copy-start(bf16[2,128,128]{2,1,0:T(8,128)(2,1)} %w2_ref.5) | copy-start | bytes 196612
  15.8 2.2 %copy-start.14 = (bf16[2,128,128]{2,1,0:T(8,128)(2,1)S(1)}, bf16[2,128,128]{2,1,0:T(8,128)(2,1)}, u32[]{:S(2)}) copy-start(bf16[2,128,128]{2,1,0:T(8,128)(2,1)} %u2_ref.5) | copy-start | bytes 196612
  15.8 2.2 %copy-start.15 = (f32[2,128]{1,0:T(2,128)S(1)}, f32[2,128]{1,0:T(2,128)}, u32[]{:S(2)}) copy-start(f32[2,128]{1,0:T(2,128)} %g1_ref.5) | copy-start | bytes 3076
  15.8 2.2 %copy-start.16 = (f32[2,128]{1,0:T(2,128)S(1)}, f32[2,128]{1,0:T(2,128)}, u32[]{:S(2)}) copy-start(f32[2,128]{1,0:T(2,128)} %g2_ref.5) | copy-start | bytes 3076
  24.0 8.2 %collective-permute-start.4 = (bf16[3,128,128]{2,1,0:T(8,128)(2,1)S(1)}, bf16[3,128,128]{2,1,0:T(8,128)(2,1)S(1)}, u32[]{:S(2)}, u32[]{:S(2)}) collective-permute-start(bf16[3,128,128]{2,1,0:T(8,128)(2,1)S(1)} %get-tuple-element.111), channel_id=1, source_target_pairs={{0,16},{32,48},{64,80},{96,112},{128,144},{160,176},{192,208},{224... | collective-permute-start | bytes 294920 | tf_op jit(solution)/shard_map/ppermute | solution.py:505
  28.9 3.3 %collective-permute-start.5 = (bf16[3,128,128]{2,1,0:T(8,128)(2,1)S(1)}, bf16[3,128,128]{2,1,0:T(8,128)(2,1)S(1)}, u32[]{:S(2)}, u32[]{:S(2)}) collective-permute-start(bf16[3,128,128]{2,1,0:T(8,128)(2,1)S(1)} %get-tuple-element.112), channel_id=1, source_target_pairs={{16,32},{48,64},{80,96},{112,128},{144,160},{176,192},{208,224},{3... | collective-permute-start | bytes 294920 | tf_op jit(solution)/shard_map/ppermute | solution.py:504
  32.3 5.9 %collective-permute-start.7 = (bf16[3,128,128]{2,1,0:T(8,128)(2,1)S(1)}, bf16[3,128,128]{2,1,0:T(8,128)(2,1)S(1)}, u32[]{:S(2)}, u32[]{:S(2)}) collective-permute-start(bf16[3,128,128]{2,1,0:T(8,128)(2,1)S(1)} %get-tuple-element.118), channel_id=1, source_target_pairs={{1,2},{3,4},{5,6},{7,8},{9,10},{11,12},{13,14},{2,1},{4,3},{6,5},{... | collective-permute-start | bytes 294920 | tf_op jit(solution)/shard_map/ppermute | solution.py:504
  36.0 2.3 %collective-permute-start.6 = (bf16[3,128,128]{2,1,0:T(8,128)(2,1)S(1)}, bf16[3,128,128]{2,1,0:T(8,128)(2,1)S(1)}, u32[]{:S(2)}, u32[]{:S(2)}) collective-permute-start(bf16[3,128,128]{2,1,0:T(8,128)(2,1)S(1)} %get-tuple-element.114), channel_id=1, source_target_pairs={{0,1},{2,3},{4,5},{6,7},{8,9},{10,11},{12,13},{14,15},{1,0},{3,2},... | collective-permute-start | bytes 294920 | tf_op jit(solution)/shard_map/ppermute | solution.py:505
  36.3 2.0 %copy-start = (bf16[1,1,4096,128]{3,2,1,0:T(8,128)(2,1)S(1)}, bf16[1,1,4096,128]{3,2,1,0:T(8,128)(2,1)}, u32[]{:S(2)}) copy-start(bf16[1,1,4096,128]{3,2,1,0:T(8,128)(2,1)} %param.21) | copy-start | bytes 3145732
  36.3 2.0 %copy-start.9 = (bf16[1,1,512,128]{3,2,1,0:T(8,128)(2,1)S(1)}, bf16[1,1,512,128]{3,2,1,0:T(8,128)(2,1)}, u32[]{:S(2)}) copy-start(bf16[1,1,512,128]{3,2,1,0:T(8,128)(2,1)} %param.20) | copy-start | bytes 393220
  38.3 14.0 %copy-start.4 = (bf16[2,384,128]{2,1,0:T(8,128)(2,1)S(1)}, bf16[2,384,128]{2,1,0:T(8,128)(2,1)}, u32[]{:S(2)}) copy-start(bf16[2,384,128]{2,1,0:T(8,128)(2,1)} %w1_ref.19) | copy-start | bytes 589828
  48.2 6.7 %collective-permute-start.8 = (bf16[3,128,128]{2,1,0:T(8,128)(2,1)S(1)}, bf16[3,128,128]{2,1,0:T(8,128)(2,1)S(1)}, u32[]{:S(2)}, u32[]{:S(2)}) collective-permute-start(bf16[3,128,128]{2,1,0:T(8,128)(2,1)S(1)} %get-tuple-element.126), channel_id=1, source_target_pairs={{0,16},{32,48},{64,80},{96,112},{128,144},{160,176},{192,208},{224... | collective-permute-start | bytes 294920 | tf_op jit(solution)/shard_map/ppermute | solution.py:505
  51.6 3.2 %collective-permute-start.9 = (bf16[3,128,128]{2,1,0:T(8,128)(2,1)S(1)}, bf16[3,128,128]{2,1,0:T(8,128)(2,1)S(1)}, u32[]{:S(2)}, u32[]{:S(2)}) collective-permute-start(bf16[3,128,128]{2,1,0:T(8,128)(2,1)S(1)} %get-tuple-element.127), channel_id=1, source_target_pairs={{16,32},{48,64},{80,96},{112,128},{144,160},{176,192},{208,224},{3... | collective-permute-start | bytes 294920 | tf_op jit(solution)/shard_map/ppermute | solution.py:504
  54.9 6.8 %collective-permute-start.10 = (bf16[3,128,128]{2,1,0:T(8,128)(2,1)S(1)}, bf16[3,128,128]{2,1,0:T(8,128)(2,1)S(1)}, u32[]{:S(2)}, u32[]{:S(2)}) collective-permute-start(bf16[3,128,128]{2,1,0:T(8,128)(2,1)S(1)} %get-tuple-element.129), channel_id=1, source_target_pairs={{0,1},{2,3},{4,5},{6,7},{8,9},{10,11},{12,13},{14,15},{1,0},{3,2},... | collective-permute-start | bytes 294920 | tf_op jit(solution)/shard_map/ppermute | solution.py:505
  55.7 5.9 %collective-permute-start.11 = (bf16[3,128,128]{2,1,0:T(8,128)(2,1)S(1)}, bf16[3,128,128]{2,1,0:T(8,128)(2,1)S(1)}, u32[]{:S(2)}, u32[]{:S(2)}) collective-permute-start(bf16[3,128,128]{2,1,0:T(8,128)(2,1)S(1)} %get-tuple-element.145), channel_id=1, source_target_pairs={{1,2},{3,4},{5,6},{7,8},{9,10},{11,12},{13,14},{2,1},{4,3},{6,5},{... | collective-permute-start | bytes 294920 | tf_op jit(solution)/shard_map/ppermute | solution.py:504
  58.8 2.8 %copy-start.11 = (bf16[1,1,512,128]{3,2,1,0:T(8,128)(2,1)S(1)}, bf16[1,1,512,128]{3,2,1,0:T(8,128)(2,1)}, u32[]{:S(2)}) copy-start(bf16[1,1,512,128]{3,2,1,0:T(8,128)(2,1)} %param.14) | copy-start | bytes 393220
  67.2 1.0 copy-start.17
  68.2 2.2 %copy-start.19 = (f32[512,128]{1,0:T(8,128)}, f32[512,128]{1,0:T(8,128)S(1)}, u32[]{:S(2)}) copy-start(f32[512,128]{1,0:T(8,128)S(1)} %get-tuple-element.168.partial_ref) | copy-start | bytes 786436
  70.3 69.2 %copy-start.6 = (s32[1,1,4096]{2,1,0:T(1,128)S(1)}, s32[1,1,4096]{2,1,0:T(1,128)}, u32[]{:S(2)}) copy-start(s32[1,1,4096]{2,1,0:T(1,128)} %param.16) | copy-start | bytes 49156
  70.3 69.2 %copy-start.8 = (s32[1,1,4096]{2,1,0:T(1,128)S(1)}, s32[1,1,4096]{2,1,0:T(1,128)}, u32[]{:S(2)}) copy-start(s32[1,1,4096]{2,1,0:T(1,128)} %param.17) | copy-start | bytes 49156
  70.3 43.4 %all-to-all-start = ((bf16[32,64,128]{2,1,0:T(8,128)(2,1)}), bf16[32,64,128]{2,1,0:T(8,128)(2,1)S(1)}, u32[]{:S(2)}, u32[]{:S(2)}) async-start(bf16[32,64,128]{2,1,0:T(8,128)(2,1)} %bitcast.8), calls=%async_computation | async-start | bytes 1048576 | tf_op jit(solution)/shard_map/all_to_all | solution.py:529
  101.7 4.2 %collective-permute-start.12 = (bf16[3,128,128]{2,1,0:T(8,128)(2,1)S(1)}, bf16[3,128,128]{2,1,0:T(8,128)(2,1)S(1)}, u32[]{:S(2)}, u32[]{:S(2)}) collective-permute-start(bf16[3,128,128]{2,1,0:T(8,128)(2,1)S(1)} %get-tuple-element.155), channel_id=1, source_target_pairs={{0,16},{32,48},{64,80},{96,112},{128,144},{160,176},{192,208},{224... | collective-permute-start | bytes 294920 | tf_op jit(solution)/shard_map/ppermute | solution.py:505
  102.1 3.8 %collective-permute-start.13 = (bf16[3,128,128]{2,1,0:T(8,128)(2,1)S(1)}, bf16[3,128,128]{2,1,0:T(8,128)(2,1)S(1)}, u32[]{:S(2)}, u32[]{:S(2)}) collective-permute-start(bf16[3,128,128]{2,1,0:T(8,128)(2,1)S(1)} %get-tuple-element.156), channel_id=1, source_target_pairs={{16,32},{48,64},{80,96},{112,128},{144,160},{176,192},{208,224},{3... | collective-permute-start | bytes 294920 | tf_op jit(solution)/shard_map/ppermute | solution.py:504
  105.9 33.6 %copy-start.20 = (f32[512,128]{1,0:T(8,128)S(1)}, f32[512,128]{1,0:T(8,128)}, u32[]{:S(2)}) copy-start(f32[512,128]{1,0:T(8,128)} %copy-done.19) | copy-start | bytes 786436
  114.5 13.0 %all-to-all-start.1 = ((bf16[8,64,128]{2,1,0:T(8,128)(2,1)}), bf16[8,64,128]{2,1,0:T(8,128)(2,1)S(1)}, u32[]{:S(2)}, u32[]{:S(2)}) async-start(bf16[8,64,128]{2,1,0:T(8,128)(2,1)} %spread.2), calls=%async_computation.1 | async-start | bytes 262144 | tf_op jit(solution)/shard_map/all_to_all | solution.py:529
  120.5 3.3 %collective-permute-start.14 = (bf16[3,128,128]{2,1,0:T(8,128)(2,1)S(1)}, bf16[3,128,128]{2,1,0:T(8,128)(2,1)S(1)}, u32[]{:S(2)}, u32[]{:S(2)}) collective-permute-start(bf16[3,128,128]{2,1,0:T(8,128)(2,1)S(1)} %get-tuple-element.163), channel_id=1, source_target_pairs={{0,1},{2,3},{4,5},{6,7},{8,9},{10,11},{12,13},{14,15},{1,0},{3,2},... | collective-permute-start | bytes 294920 | tf_op jit(solution)/shard_map/ppermute | solution.py:505
  121.2 6.2 %collective-permute-start.15 = (bf16[3,128,128]{2,1,0:T(8,128)(2,1)S(1)}, bf16[3,128,128]{2,1,0:T(8,128)(2,1)S(1)}, u32[]{:S(2)}, u32[]{:S(2)}) collective-permute-start(bf16[3,128,128]{2,1,0:T(8,128)(2,1)S(1)} %get-tuple-element.164), channel_id=1, source_target_pairs={{1,2},{3,4},{5,6},{7,8},{9,10},{11,12},{13,14},{2,1},{4,3},{6,5},{... | collective-permute-start | bytes 294920 | tf_op jit(solution)/shard_map/ppermute | solution.py:504
  128.3 22.7 %all-to-all-start.2 = ((bf16[32,64,128]{2,1,0:T(8,128)(2,1)}), bf16[32,64,128]{2,1,0:T(8,128)(2,1)S(1)}, u32[]{:S(2)}, u32[]{:S(2)}) async-start(bf16[32,64,128]{2,1,0:T(8,128)(2,1)} %spread.3), calls=%async_computation.2 | async-start | bytes 1048576 | tf_op jit(solution)/shard_map/all_to_all | solution.py:529
  139.6 1.2 copy-start.18
where the time goes:
time: 153 us; the launch traced here: 152 us
  starting transfers between devices  77.7 us (51%)
  Pallas kernels  42.3 us (28%)
  waiting for transfers between devices  22.9 us (15%)
  local copies, waits for them, and re-layouts  7.44 us (5%)
  between operations  1.68 us (1%)
    all_to_all x3, starting transfers between devices, trade(): lax.all_to_all(parts, axes, 0, 0, tiled=True, axis_index_groups=groups)  48.5 us
    pallas_call x20, Pallas kernels, call(): pl.pallas_call(kernel, name=name, out_shape=[jax.ShapeDtypeStruct(s, d) f...  42.3 us
    ppermute x8, starting transfers between devices, swap(): odd = lax.ppermute(to_odd, axis, pairs(1))  15.9 us
    ppermute x8, starting transfers between devices, swap(): return (lax.ppermute(to_even, axis, pairs(0)), odd)  13.3 us
    all_to_all x3, waiting for transfers between devices, trade(): lax.all_to_all(parts, axes, 0, 0, tiled=True, axis_index_groups=groups)  12.5 us
    unnamed x43, local copies, waits for them, and re-layouts  7.44 us
    ppermute x8, waiting for transfers between devices, swap(): odd = lax.ppermute(to_odd, axis, pairs(1))  5.6 us
    ppermute x8, waiting for transfers between devices, swap(): return (lax.ppermute(to_even, axis, pairs(0)), odd)  4.87 us
  transfers between devices with their start and end apart: 19, of which 9 were waited for; matrix products, arithmetic and copies ran while one was open for 0% of the time, Pallas kernels for 10%

commit v1 on v0

--- a/solution.py
+++ b/solution.py
@@ -675,10 +675,10 @@
         weights_kernel, "weights", [((LAYERS * PACKED, L), BF16)], [dw1_f, dw2_f], 0, 2 * 10**9,
         sent_0, *received_0, edges0, z_0, dy, dz, sums, packed1
     )
-    total, returned, dsent = sum_over_domains(packed, ghost_grad, dsent)
+    total, returned, held_ids = sum_over_domains(packed, ghost_grad, ids)
     edge_grad, partial = call(
         shares_kernel, "shares", [edge_f, node_f], [dlocal_f, dtile_f, dtile_f], 0, 2 * 10**9, dz,
-        dsent, ids, targets, edge_first, edge_grad0, edge_grad1, partial
+        dsent, held_ids, targets, edge_first, edge_grad0, edge_grad1, partial
     )
     (node_grad,) = call(
         return_kernel, "returned", [node_f], [], 0, 10**8, partial, grow, *returned

time: 153 us -> 153 us (level)
  no operation moved by 1% of the time
where the time goes in v1:
time: 153 us; the launch traced here: 152 us
  starting transfers between devices  77.7 us (51%)
  Pallas kernels  42.3 us (28%)
  waiting for transfers between devices  22.9 us (15%)
  local copies, waits for them, and re-layouts  7.44 us (5%)
  between operations  1.68 us (1%)
    all_to_all x3, starting transfers between devices, trade(): lax.all_to_all(parts, axes, 0, 0, tiled=True, axis_index_groups=groups)  48.5 us
    pallas_call x20, Pallas kernels, call(): pl.pallas_call(kernel, name=name, out_shape=[jax.ShapeDtypeStruct(s, d) f...  42.3 us
    ppermute x8, starting transfers between devices, swap(): odd = lax.ppermute(to_odd, axis, pairs(1))  15.9 us
    ppermute x8, starting transfers between devices, swap(): return (lax.ppermute(to_even, axis, pairs(0)), odd)  13.3 us
    all_to_all x3, waiting for transfers between devices, trade(): lax.all_to_all(parts, axes, 0, 0, tiled=True, axis_index_groups=groups)  12.5 us
    unnamed x43, local copies, waits for them, and re-layouts  7.44 us
    ppermute x8, waiting for transfers between devices, swap(): odd = lax.ppermute(to_odd, axis, pairs(1))  5.6 us
    ppermute x8, waiting for transfers between devices, swap(): return (lax.ppermute(to_even, axis, pairs(0)), odd)  4.87 us
  transfers between devices with their start and end apart: 19, of which 9 were waited for; matrix products, arithmetic and copies ran while one was open for 0% of the time, Pallas kernels for 10%

profile of v1, /device:TPU:1, one launch (start us, length us, event | category | flops | bytes accessed | tf_op | source)
XLA Modules:
  0.0 152.0 jit_solution(6142450993714693227)
XLA Ops:
  0.6 0.7 copy.26
  1.3 0.9 copy-done.10
  2.2 0.5 pick.1
  2.7 2.6 %collective-permute-start = (bf16[3,128,128]{2,1,0:T(8,128)(2,1)S(1)}, bf16[3,128,128]{2,1,0:T(8,128)(2,1)S(1)}, u32[]{:S(2)}, u32[]{:S(2)}) collective-permute-start(bf16[3,128,128]{2,1,0:T(8,128)(2,1)S(1)} %get-tuple-element.98), channel_id=1, source_target_pairs={{0,16},{32,48},{64,80},{96,112},{128,144},{160,176},{192,208},{224... | collective-permute-start | bytes 294920 | tf_op jit(solution)/shard_map/ppermute | solution.py:505
  5.3 0.7 collective-permute-start.1
  6.6 0.0 copy-start.1
  6.6 1.2 copy-done.1
  7.8 0.9 copy-done.3
  8.8 0.7 copy-done.5
  9.5 0.7 copy-done.7
  10.2 1.4 before00.1
  11.6 0.1 turn.4
  11.7 4.0 %collective-permute-start.3 = (bf16[3,128,128]{2,1,0:T(8,128)(2,1)S(1)}, bf16[3,128,128]{2,1,0:T(8,128)(2,1)S(1)}, u32[]{:S(2)}, u32[]{:S(2)}) collective-permute-start(bf16[3,128,128]{2,1,0:T(8,128)(2,1)S(1)} %get-tuple-element.105), channel_id=1, source_target_pairs={{1,2},{3,4},{5,6},{7,8},{9,10},{11,12},{13,14},{2,1},{4,3},{6,5},{... | collective-permute-start | bytes 294920 | tf_op jit(solution)/shard_map/ppermute | solution.py:504
  15.7 0.1 collective-permute-start.2
  15.8 0.0 copy-start.12
  15.8 0.0 copy-start.15
  15.8 0.0 copy-start.16
  15.8 1.4 before01.1
  17.3 0.7 collective-permute-done.3.rest_3_
  18.0 6.0 %first.1 = (bf16[512,128]{1,0:T(8,128)(2,1)S(1)}, bf16[512,128]{1,0:T(8,128)(2,1)S(1)}, bf16[3,128,128]{2,1,0:T(8,128)(2,1)S(1)}, bf16[3,128,128]{2,1,0:T(8,128)...) custom-call(s32[1,1]{1,0:T(1,128)S(6)} %copy.27.count_ref, ...), custom_call_target="tpu_custom_call" | custom-call | flops 4000000000 | bytes 1048576 | tf_op jit(solution)/shard_map/first/pallas_call | solution.py:487
  24.0 4.9 %collective-permute-start.4 = (bf16[3,128,128]{2,1,0:T(8,128)(2,1)S(1)}, bf16[3,128,128]{2,1,0:T(8,128)(2,1)S(1)}, u32[]{:S(2)}, u32[]{:S(2)}) collective-permute-start(bf16[3,128,128]{2,1,0:T(8,128)(2,1)S(1)} %get-tuple-element.111), channel_id=1, source_target_pairs={{0,16},{32,48},{64,80},{96,112},{128,144},{160,176},{192,208},{224... | collective-permute-start | bytes 294920 | tf_op jit(solution)/shard_map/ppermute | solution.py:505
  28.9 0.7 collective-permute-start.5
  29.6 1.4 before10.1
  31.0 1.3 collective-permute-done.4.even_x.rest_0_
  32.3 0.1 turn.5
  32.3 3.7 %collective-permute-start.7 = (bf16[3,128,128]{2,1,0:T(8,128)(2,1)S(1)}, bf16[3,128,128]{2,1,0:T(8,128)(2,1)S(1)}, u32[]{:S(2)}, u32[]{:S(2)}) collective-permute-start(bf16[3,128,128]{2,1,0:T(8,128)(2,1)S(1)} %get-tuple-element.118), channel_id=1, source_target_pairs={{1,2},{3,4},{5,6},{7,8},{9,10},{11,12},{13,14},{2,1},{4,3},{6,5},{... | collective-permute-start | bytes 294920 | tf_op jit(solution)/shard_map/ppermute | solution.py:504
  36.0 0.3 collective-permute-start.6
  36.3 0.0 copy-start
  36.3 1.4 before11.1
  37.7 0.5 collective-permute-done.7.rest_3_
  38.3 0.0 copy-start.4
  38.3 9.9 %middle.1 = (bf16[512,128]{1,0:T(8,128)(2,1)}, bf16[4096,128]{1,0:T(8,128)(2,1)}, bf16[4096,128]{1,0:T(8,128)(2,1)S(1)}, f32[4096,128]{1,0:T(8,128)S(1)}, bf16[4...) custom-call(s32[1,1]{1,0:T(1,128)S(6)} %copy.27.count_ref, ...), custom_call_target="tpu_custom_call" | custom-call | flops 8000000000 | bytes 1048576 | tf_op jit(solution)/shard_map/middle/pallas_call | solution.py:487
  48.2 3.5 %collective-permute-start.8 = (bf16[3,128,128]{2,1,0:T(8,128)(2,1)S(1)}, bf16[3,128,128]{2,1,0:T(8,128)(2,1)S(1)}, u32[]{:S(2)}, u32[]{:S(2)}) collective-permute-start(bf16[3,128,128]{2,1,0:T(8,128)(2,1)S(1)} %get-tuple-element.126), channel_id=1, source_target_pairs={{0,16},{32,48},{64,80},{96,112},{128,144},{160,176},{192,208},{224... | collective-permute-start | bytes 294920 | tf_op jit(solution)/shard_map/ppermute | solution.py:505
  51.6 0.7 collective-permute-start.9
  52.3 2.1 %after10.1 = (bf16[2048,128]{1,0:T(8,128)(2,1)S(1)}, f32[384,128]{1,0:T(8,128)S(1)}, f32[128,128]{1,0:T(8,128)S(1)}, f32[256,256]{1,0:T(8,128)S(1)}, f32[256,128]{1,0:T(8,128)S(1)}) custom-call(bf16[4096,128]{1,0:T(8,128)(2,1)S(1)} %get-tuple-element.122.sent_ref, bf16[2048,128]{1,0:T(8,128)(2,1)S(1)} %get-tuple-element.110.received_ref, ...), custom_call_target="tpu_custom_call" | custom-call | flops 2000000000 | bytes 1048576 | tf_op jit(solution)/shard_map/after10/pallas_call | solution.py:487
  54.3 0.5 collective-permute-done.8.even_x.rest_0_
  54.8 0.1 turn.6
  54.9 0.8 collective-permute-start.10
  55.7 3.1 %collective-permute-start.11 = (bf16[3,128,128]{2,1,0:T(8,128)(2,1)S(1)}, bf16[3,128,128]{2,1,0:T(8,128)(2,1)S(1)}, u32[]{:S(2)}, u32[]{:S(2)}) collective-permute-start(bf16[3,128,128]{2,1,0:T(8,128)(2,1)S(1)} %get-tuple-element.145), channel_id=1, source_target_pairs={{1,2},{3,4},{5,6},{7,8},{9,10},{11,12},{13,14},{2,1},{4,3},{6,5},{... | collective-permute-start | bytes 294920 | tf_op jit(solution)/shard_map/ppermute | solution.py:504
  58.9 2.1 %after11.1 = (bf16[2048,128]{1,0:T(8,128)(2,1)S(1)}, f32[512,128]{1,0:T(8,128)S(1)}, bf16[1024,128]{1,0:T(8,128)(2,1)S(1)}) custom-call(bf16[4096,128]{1,0:T(8,128)(2,1)S(1)} %get-tuple-element.122.sent_ref, bf16[2048,128]{1,0:T(8,128)(2,1)S(1)} %get-tuple-element.123.received_ref, bf16[4096,128]{1,0:T(8,128)(2,1)S(1)} %get-tuple-element.107.edges_ref, ...), custom_call_target="tpu_custom_call" | custom-call | flops 2000000000 | bytes 1048576 | tf_op jit(solution)/shard_map/after11/pallas_call | solution.py:487
  61.0 0.7 collective-permute-done.11.rest_3_
  61.7 5.5 %last.1 = (bf16[4096,128]{1,0:T(8,128)(2,1)S(1)}, bf16[4096,128]{1,0:T(8,128)(2,1)S(1)}, bf16[4096,128]{1,0:T(8,128)(2,1)S(1)}, f32[512,128]{1,0:T(8,128)S(1)}, ...) custom-call(s32[1,1]{1,0:T(1,128)S(6)} %copy.27.count_ref, ...), custom_call_target="tpu_custom_call" | custom-call | flops 4000000000 | bytes 1048576 | tf_op jit(solution)/shard_map/last/pallas_call | solution.py:487
  67.2 0.0 copy-start.17
  67.2 1.0 copy-done.17
  68.2 2.2 %weights.1 = bf16[2048,128]{1,0:T(8,128)(2,1)} custom-call(bf16[4096,128]{1,0:T(8,128)(2,1)S(1)} %get-tuple-element.148.sent_ref, bf16[2048,128]{1,0:T(8,128)(2,1)S(1)} %get-tuple-element.97.received0, bf16[2048,128]{1,0:T(8,128)(2,1)S(1)} %get-tuple-element.149.received1, bf16[4096,128]{1,0:T(8,128)(2,1)S(1)} %bitcast.22, ...), custom_call_target="tpu_custom_call" | custom-call | flops 2000000000 | bytes 1048576 | tf_op jit(solution)/shard_map/weights/pallas_call | solution.py:487
  70.3 31.3 %all-to-all-start = ((bf16[32,64,128]{2,1,0:T(8,128)(2,1)}), bf16[32,64,128]{2,1,0:T(8,128)(2,1)S(1)}, u32[]{:S(2)}, u32[]{:S(2)}) async-start(bf16[32,64,128]{2,1,0:T(8,128)(2,1)} %bitcast.8), calls=%async_computation | async-start | bytes 1048576 | tf_op jit(solution)/shard_map/all_to_all | solution.py:529
  101.7 0.5 collective-permute-start.12
  102.1 0.7 collective-permute-start.13
  102.8 3.1 %collective-permute-done.12.even_x.rest_0_ = bf16[3,128,128]{2,1,0:T(8,128)(2,1)S(1)} collective-permute-done((bf16[3,128,128]{2,1,0:T(8,128)(2,1)S(1)}, bf16[3,128,128]{2,1,0:T(8,128)(2,1)S(1)}, u32[]{:S(2)}, u32[]{:S(2)}) %collective-permute-start.12) | collective-permute-done | bytes 98336 | tf_op jit(solution)/shard_map/ppermute | solution.py:505
  105.9 7.8 %all-to-all-done.parts_ref = bf16[32,64,128]{2,1,0:T(8,128)(2,1)S(1)} async-done(((bf16[32,64,128]{2,1,0:T(8,128)(2,1)}), bf16[32,64,128]{2,1,0:T(8,128)(2,1)S(1)}, u32[]{:S(2)}, u32[]{:S(2)}) %all-to-all-start) | async-done | bytes 524320 | tf_op jit(solution)/shard_map/all_to_all | solution.py:529
  113.7 0.7 spread.2
  114.5 6.0 %all-to-all-start.1 = ((bf16[8,64,128]{2,1,0:T(8,128)(2,1)}), bf16[8,64,128]{2,1,0:T(8,128)(2,1)S(1)}, u32[]{:S(2)}, u32[]{:S(2)}) async-start(bf16[8,64,128]{2,1,0:T(8,128)(2,1)} %spread.2), calls=%async_computation.1 | async-start | bytes 262144 | tf_op jit(solution)/shard_map/all_to_all | solution.py:529
  120.5 0.1 turn.7
  120.5 0.7 collective-permute-start.14
  121.2 2.5 %collective-permute-start.15 = (bf16[3,128,128]{2,1,0:T(8,128)(2,1)S(1)}, bf16[3,128,128]{2,1,0:T(8,128)(2,1)S(1)}, u32[]{:S(2)}, u32[]{:S(2)}) collective-permute-start(bf16[3,128,128]{2,1,0:T(8,128)(2,1)S(1)} %get-tuple-element.165), channel_id=1, source_target_pairs={{1,2},{3,4},{5,6},{7,8},{9,10},{11,12},{13,14},{2,1},{4,3},{6,5},{... | collective-permute-start | bytes 294920 | tf_op jit(solution)/shard_map/ppermute | solution.py:504
  123.8 3.7 %collective-permute-done.15.rest_3_ = bf16[3,128,128]{2,1,0:T(8,128)(2,1)S(1)} collective-permute-done((bf16[3,128,128]{2,1,0:T(8,128)(2,1)S(1)}, bf16[3,128,128]{2,1,0:T(8,128)(2,1)S(1)}, u32[]{:S(2)}, u32[]{:S(2)}) %collective-permute-start.15) | collective-permute-done | bytes 98336 | tf_op jit(solution)/shard_map/ppermute | solution.py:504
  127.5 0.9 spread.3
  128.3 11.2 %all-to-all-start.2 = ((bf16[32,64,128]{2,1,0:T(8,128)(2,1)}), bf16[32,64,128]{2,1,0:T(8,128)(2,1)S(1)}, u32[]{:S(2)}, u32[]{:S(2)}) async-start(bf16[32,64,128]{2,1,0:T(8,128)(2,1)} %spread.3), calls=%async_computation.2 | async-start | bytes 1048576 | tf_op jit(solution)/shard_map/all_to_all | solution.py:529
  139.6 0.0 copy-start.18
  139.6 1.2 copy-done.18
  140.8 4.5 %shares.1 = (f32[4096,128]{1,0:T(8,128)}, f32[512,128]{1,0:T(8,128)S(1)}) custom-call(bf16[4096,128]{1,0:T(8,128)(2,1)S(1)} %get-tuple-element.146.dz_ref, bf16[4096,128]{1,0:T(8,128)(2,1)S(1)} %copy-done.18, s32[1,4096]{1,0:T(1,128)S(1)} %bitcast.32, s32[1,4096]{1,0:T(1,128)S(1)} %bitcast.42, bf16[2,384,128]{2,1,0:T(8,128)(2,1)S(1)} %copy-done.4, ...), custom_call_target="tpu_custom_call" | custom-call | flops 2000000000 | bytes 1048576 | tf_op jit(solution)/shard_map/shares/pallas_call | solution.py:487
  145.2 1.2 returned.1
  146.4 4.7 %all-to-all-done.2 = bf16[32,64,128]{2,1,0:T(8,128)(2,1)S(1)} async-done(((bf16[32,64,128]{2,1,0:T(8,128)(2,1)}), bf16[32,64,128]{2,1,0:T(8,128)(2,1)S(1)}, u32[]{:S(2)}, u32[]{:S(2)}) %all-to-all-start.2) | async-done | bytes 524320 | tf_op jit(solution)/shard_map/all_to_all | solution.py:529
  151.1 0.9 unpack.1
  (37 shorter events, 0.1 us)
Async XLA Ops:
  1.3 0.9 copy-start.10
  2.7 8.9 %collective-permute-start = (bf16[3,128,128]{2,1,0:T(8,128)(2,1)S(1)}, bf16[3,128,128]{2,1,0:T(8,128)(2,1)S(1)}, u32[]{:S(2)}, u32[]{:S(2)}) collective-permute-start(bf16[3,128,128]{2,1,0:T(8,128)(2,1)S(1)} %get-tuple-element.98), channel_id=1, source_target_pairs={{0,16},{32,48},{64,80},{96,112},{128,144},{160,176},{192,208},{224... | collective-permute-start | bytes 294920 | tf_op jit(solution)/shard_map/ppermute | solution.py:505
  5.3 6.3 %collective-permute-start.1 = (bf16[3,128,128]{2,1,0:T(8,128)(2,1)S(1)}, bf16[3,128,128]{2,1,0:T(8,128)(2,1)S(1)}, u32[]{:S(2)}, u32[]{:S(2)}) collective-permute-start(bf16[3,128,128]{2,1,0:T(8,128)(2,1)S(1)} %get-tuple-element.99), channel_id=1, source_target_pairs={{16,32},{48,64},{80,96},{112,128},{144,160},{176,192},{208,224},{3... | collective-permute-start | bytes 294920 | tf_op jit(solution)/shard_map/ppermute | solution.py:504
  6.6 1.2 copy-start.1
  7.8 0.9 copy-start.3
  8.8 0.7 copy-start.5
  9.5 0.7 copy-start.7
  10.2 5.6 %copy-start.2 = (bf16[1,1,4096,128]{3,2,1,0:T(8,128)(2,1)S(1)}, bf16[1,1,4096,128]{3,2,1,0:T(8,128)(2,1)}, u32[]{:S(2)}) copy-start(bf16[1,1,4096,128]{3,2,1,0:T(8,128)(2,1)} %param.15) | copy-start | bytes 3145732
  11.7 6.2 %collective-permute-start.3 = (bf16[3,128,128]{2,1,0:T(8,128)(2,1)S(1)}, bf16[3,128,128]{2,1,0:T(8,128)(2,1)S(1)}, u32[]{:S(2)}, u32[]{:S(2)}) collective-permute-start(bf16[3,128,128]{2,1,0:T(8,128)(2,1)S(1)} %get-tuple-element.105), channel_id=1, source_target_pairs={{1,2},{3,4},{5,6},{7,8},{9,10},{11,12},{13,14},{2,1},{4,3},{6,5},{... | collective-permute-start | bytes 294920 | tf_op jit(solution)/shard_map/ppermute | solution.py:504
  15.7 2.3 %collective-permute-start.2 = (bf16[3,128,128]{2,1,0:T(8,128)(2,1)S(1)}, bf16[3,128,128]{2,1,0:T(8,128)(2,1)S(1)}, u32[]{:S(2)}, u32[]{:S(2)}) collective-permute-start(bf16[3,128,128]{2,1,0:T(8,128)(2,1)S(1)} %get-tuple-element.101), channel_id=1, source_target_pairs={{0,1},{2,3},{4,5},{6,7},{8,9},{10,11},{12,13},{14,15},{1,0},{3,2},... | collective-permute-start | bytes 294920 | tf_op jit(solution)/shard_map/ppermute | solution.py:505
  15.8 2.2 %copy-start.12 = (bf16[2,256,128]{2,1,0:T(8,128)(2,1)S(1)}, bf16[2,256,128]{2,1,0:T(8,128)(2,1)}, u32[]{:S(2)}) copy-start(bf16[2,256,128]{2,1,0:T(8,128)(2,1)} %u1_ref.5) | copy-start | bytes 393220
  15.8 2.2 %copy-start.13 = (bf16[2,128,128]{2,1,0:T(8,128)(2,1)S(1)}, bf16[2,128,128]{2,1,0:T(8,128)(2,1)}, u32[]{:S(2)}) copy-start(bf16[2,128,128]{2,1,0:T(8,128)(2,1)} %w2_ref.5) | copy-start | bytes 196612
  15.8 2.2 %copy-start.14 = (bf16[2,128,128]{2,1,0:T(8,128)(2,1)S(1)}, bf16[2,128,128]{2,1,0:T(8,128)(2,1)}, u32[]{:S(2)}) copy-start(bf16[2,128,128]{2,1,0:T(8,128)(2,1)} %u2_ref.5) | copy-start | bytes 196612
  15.8 2.2 %copy-start.15 = (f32[2,128]{1,0:T(2,128)S(1)}, f32[2,128]{1,0:T(2,128)}, u32[]{:S(2)}) copy-start(f32[2,128]{1,0:T(2,128)} %g1_ref.5) | copy-start | bytes 3076
  15.8 2.2 %copy-start.16 = (f32[2,128]{1,0:T(2,128)S(1)}, f32[2,128]{1,0:T(2,128)}, u32[]{:S(2)}) copy-start(f32[2,128]{1,0:T(2,128)} %g2_ref.5) | copy-start | bytes 3076
  24.0 8.2 %collective-permute-start.4 = (bf16[3,128,128]{2,1,0:T(8,128)(2,1)S(1)}, bf16[3,128,128]{2,1,0:T(8,128)(2,1)S(1)}, u32[]{:S(2)}, u32[]{:S(2)}) collective-permute-start(bf16[3,128,128]{2,1,0:T(8,128)(2,1)S(1)} %get-tuple-element.111), channel_id=1, source_target_pairs={{0,16},{32,48},{64,80},{96,112},{128,144},{160,176},{192,208},{224... | collective-permute-start | bytes 294920 | tf_op jit(solution)/shard_map/ppermute | solution.py:505
  28.9 3.3 %collective-permute-start.5 = (bf16[3,128,128]{2,1,0:T(8,128)(2,1)S(1)}, bf16[3,128,128]{2,1,0:T(8,128)(2,1)S(1)}, u32[]{:S(2)}, u32[]{:S(2)}) collective-permute-start(bf16[3,128,128]{2,1,0:T(8,128)(2,1)S(1)} %get-tuple-element.112), channel_id=1, source_target_pairs={{16,32},{48,64},{80,96},{112,128},{144,160},{176,192},{208,224},{3... | collective-permute-start | bytes 294920 | tf_op jit(solution)/shard_map/ppermute | solution.py:504
  32.3 5.9 %collective-permute-start.7 = (bf16[3,128,128]{2,1,0:T(8,128)(2,1)S(1)}, bf16[3,128,128]{2,1,0:T(8,128)(2,1)S(1)}, u32[]{:S(2)}, u32[]{:S(2)}) collective-permute-start(bf16[3,128,128]{2,1,0:T(8,128)(2,1)S(1)} %get-tuple-element.118), channel_id=1, source_target_pairs={{1,2},{3,4},{5,6},{7,8},{9,10},{11,12},{13,14},{2,1},{4,3},{6,5},{... | collective-permute-start | bytes 294920 | tf_op jit(solution)/shard_map/ppermute | solution.py:504
  36.0 2.3 %collective-permute-start.6 = (bf16[3,128,128]{2,1,0:T(8,128)(2,1)S(1)}, bf16[3,128,128]{2,1,0:T(8,128)(2,1)S(1)}, u32[]{:S(2)}, u32[]{:S(2)}) collective-permute-start(bf16[3,128,128]{2,1,0:T(8,128)(2,1)S(1)} %get-tuple-element.114), channel_id=1, source_target_pairs={{0,1},{2,3},{4,5},{6,7},{8,9},{10,11},{12,13},{14,15},{1,0},{3,2},... | collective-permute-start | bytes 294920 | tf_op jit(solution)/shard_map/ppermute | solution.py:505
  36.3 2.0 %copy-start = (bf16[1,1,4096,128]{3,2,1,0:T(8,128)(2,1)S(1)}, bf16[1,1,4096,128]{3,2,1,0:T(8,128)(2,1)}, u32[]{:S(2)}) copy-start(bf16[1,1,4096,128]{3,2,1,0:T(8,128)(2,1)} %param.21) | copy-start | bytes 3145732
  36.3 2.0 %copy-start.9 = (bf16[1,1,512,128]{3,2,1,0:T(8,128)(2,1)S(1)}, bf16[1,1,512,128]{3,2,1,0:T(8,128)(2,1)}, u32[]{:S(2)}) copy-start(bf16[1,1,512,128]{3,2,1,0:T(8,128)(2,1)} %param.20) | copy-start | bytes 393220
  38.3 14.0 %copy-start.4 = (bf16[2,384,128]{2,1,0:T(8,128)(2,1)S(1)}, bf16[2,384,128]{2,1,0:T(8,128)(2,1)}, u32[]{:S(2)}) copy-start(bf16[2,384,128]{2,1,0:T(8,128)(2,1)} %w1_ref.19) | copy-start | bytes 589828
  48.2 6.7 %collective-permute-start.8 = (bf16[3,128,128]{2,1,0:T(8,128)(2,1)S(1)}, bf16[3,128,128]{2,1,0:T(8,128)(2,1)S(1)}, u32[]{:S(2)}, u32[]{:S(2)}) collective-permute-start(bf16[3,128,128]{2,1,0:T(8,128)(2,1)S(1)} %get-tuple-element.126), channel_id=1, source_target_pairs={{0,16},{32,48},{64,80},{96,112},{128,144},{160,176},{192,208},{224... | collective-permute-start | bytes 294920 | tf_op jit(solution)/shard_map/ppermute | solution.py:505
  51.6 3.2 %collective-permute-start.9 = (bf16[3,128,128]{2,1,0:T(8,128)(2,1)S(1)}, bf16[3,128,128]{2,1,0:T(8,128)(2,1)S(1)}, u32[]{:S(2)}, u32[]{:S(2)}) collective-permute-start(bf16[3,128,128]{2,1,0:T(8,128)(2,1)S(1)} %get-tuple-element.127), channel_id=1, source_target_pairs={{16,32},{48,64},{80,96},{112,128},{144,160},{176,192},{208,224},{3... | collective-permute-start | bytes 294920 | tf_op jit(solution)/shard_map/ppermute | solution.py:504
  54.9 6.8 %collective-permute-start.10 = (bf16[3,128,128]{2,1,0:T(8,128)(2,1)S(1)}, bf16[3,128,128]{2,1,0:T(8,128)(2,1)S(1)}, u32[]{:S(2)}, u32[]{:S(2)}) collective-permute-start(bf16[3,128,128]{2,1,0:T(8,128)(2,1)S(1)} %get-tuple-element.129), channel_id=1, source_target_pairs={{0,1},{2,3},{4,5},{6,7},{8,9},{10,11},{12,13},{14,15},{1,0},{3,2},... | collective-permute-start | bytes 294920 | tf_op jit(solution)/shard_map/ppermute | solution.py:505
  55.7 5.9 %collective-permute-start.11 = (bf16[3,128,128]{2,1,0:T(8,128)(2,1)S(1)}, bf16[3,128,128]{2,1,0:T(8,128)(2,1)S(1)}, u32[]{:S(2)}, u32[]{:S(2)}) collective-permute-start(bf16[3,128,128]{2,1,0:T(8,128)(2,1)S(1)} %get-tuple-element.145), channel_id=1, source_target_pairs={{1,2},{3,4},{5,6},{7,8},{9,10},{11,12},{13,14},{2,1},{4,3},{6,5},{... | collective-permute-start | bytes 294920 | tf_op jit(solution)/shard_map/ppermute | solution.py:504
  58.8 2.8 %copy-start.11 = (bf16[1,1,512,128]{3,2,1,0:T(8,128)(2,1)S(1)}, bf16[1,1,512,128]{3,2,1,0:T(8,128)(2,1)}, u32[]{:S(2)}) copy-start(bf16[1,1,512,128]{3,2,1,0:T(8,128)(2,1)} %param.14) | copy-start | bytes 393220
  67.2 1.0 copy-start.17
  68.2 2.2 %copy-start.19 = (f32[512,128]{1,0:T(8,128)}, f32[512,128]{1,0:T(8,128)S(1)}, u32[]{:S(2)}) copy-start(f32[512,128]{1,0:T(8,128)S(1)} %get-tuple-element.168.partial_ref) | copy-start | bytes 786436
  70.3 69.2 %copy-start.6 = (s32[1,1,4096]{2,1,0:T(1,128)S(1)}, s32[1,1,4096]{2,1,0:T(1,128)}, u32[]{:S(2)}) copy-start(s32[1,1,4096]{2,1,0:T(1,128)} %param.16) | copy-start | bytes 49156
  70.3 69.2 %copy-start.8 = (s32[1,1,4096]{2,1,0:T(1,128)S(1)}, s32[1,1,4096]{2,1,0:T(1,128)}, u32[]{:S(2)}) copy-start(s32[1,1,4096]{2,1,0:T(1,128)} %param.17) | copy-start | bytes 49156
  70.3 43.4 %all-to-all-start = ((bf16[32,64,128]{2,1,0:T(8,128)(2,1)}), bf16[32,64,128]{2,1,0:T(8,128)(2,1)S(1)}, u32[]{:S(2)}, u32[]{:S(2)}) async-start(bf16[32,64,128]{2,1,0:T(8,128)(2,1)} %bitcast.8), calls=%async_computation | async-start | bytes 1048576 | tf_op jit(solution)/shard_map/all_to_all | solution.py:529
  101.7 4.2 %collective-permute-start.12 = (bf16[3,128,128]{2,1,0:T(8,128)(2,1)S(1)}, bf16[3,128,128]{2,1,0:T(8,128)(2,1)S(1)}, u32[]{:S(2)}, u32[]{:S(2)}) collective-permute-start(bf16[3,128,128]{2,1,0:T(8,128)(2,1)S(1)} %get-tuple-element.156), channel_id=1, source_target_pairs={{0,16},{32,48},{64,80},{96,112},{128,144},{160,176},{192,208},{224... | collective-permute-start | bytes 294920 | tf_op jit(solution)/shard_map/ppermute | solution.py:505
  102.1 3.8 %collective-permute-start.13 = (bf16[3,128,128]{2,1,0:T(8,128)(2,1)S(1)}, bf16[3,128,128]{2,1,0:T(8,128)(2,1)S(1)}, u32[]{:S(2)}, u32[]{:S(2)}) collective-permute-start(bf16[3,128,128]{2,1,0:T(8,128)(2,1)S(1)} %get-tuple-element.157), channel_id=1, source_target_pairs={{16,32},{48,64},{80,96},{112,128},{144,160},{176,192},{208,224},{3... | collective-permute-start | bytes 294920 | tf_op jit(solution)/shard_map/ppermute | solution.py:504
  105.9 33.6 %copy-start.20 = (f32[512,128]{1,0:T(8,128)S(1)}, f32[512,128]{1,0:T(8,128)}, u32[]{:S(2)}) copy-start(f32[512,128]{1,0:T(8,128)} %copy-done.19) | copy-start | bytes 786436
  114.5 13.0 %all-to-all-start.1 = ((bf16[8,64,128]{2,1,0:T(8,128)(2,1)}), bf16[8,64,128]{2,1,0:T(8,128)(2,1)S(1)}, u32[]{:S(2)}, u32[]{:S(2)}) async-start(bf16[8,64,128]{2,1,0:T(8,128)(2,1)} %spread.2), calls=%async_computation.1 | async-start | bytes 262144 | tf_op jit(solution)/shard_map/all_to_all | solution.py:529
  120.5 3.3 %collective-permute-start.14 = (bf16[3,128,128]{2,1,0:T(8,128)(2,1)S(1)}, bf16[3,128,128]{2,1,0:T(8,128)(2,1)S(1)}, u32[]{:S(2)}, u32[]{:S(2)}) collective-permute-start(bf16[3,128,128]{2,1,0:T(8,128)(2,1)S(1)} %get-tuple-element.164), channel_id=1, source_target_pairs={{0,1},{2,3},{4,5},{6,7},{8,9},{10,11},{12,13},{14,15},{1,0},{3,2},... | collective-permute-start | bytes 294920 | tf_op jit(solution)/shard_map/ppermute | solution.py:505
  121.2 6.2 %collective-permute-start.15 = (bf16[3,128,128]{2,1,0:T(8,128)(2,1)S(1)}, bf16[3,128,128]{2,1,0:T(8,128)(2,1)S(1)}, u32[]{:S(2)}, u32[]{:S(2)}) collective-permute-start(bf16[3,128,128]{2,1,0:T(8,128)(2,1)S(1)} %get-tuple-element.165), channel_id=1, source_target_pairs={{1,2},{3,4},{5,6},{7,8},{9,10},{11,12},{13,14},{2,1},{4,3},{6,5},{... | collective-permute-start | bytes 294920 | tf_op jit(solution)/shard_map/ppermute | solution.py:504
  128.3 22.7 %all-to-all-start.2 = ((bf16[32,64,128]{2,1,0:T(8,128)(2,1)}), bf16[32,64,128]{2,1,0:T(8,128)(2,1)S(1)}, u32[]{:S(2)}, u32[]{:S(2)}) async-start(bf16[32,64,128]{2,1,0:T(8,128)(2,1)} %spread.3), calls=%async_computation.2 | async-start | bytes 1048576 | tf_op jit(solution)/shard_map/all_to_all | solution.py:529
  139.6 1.2 copy-start.18
